TPU v7x, 256 devices: a whole 4x4x8 slice. The times are simulated.
256 devices in a mesh: dp: 64 (over x_lo, y, z), mp: 4 (over x_hi, core).
Axes of the slice: x: 4 (x_hi: 2, x_lo: 2; x = x_hi * 2 + x_lo), y: 4, z: 8, core: 2. Of those that a mesh axis runs over, the one named last changes fastest.
Arguments:
- activations: bfloat16 [16384, 2560], P('dp', 'mp'), may hold values from -6 to 6
- grad_out: bfloat16 [16384, 5120], P('dp', 'mp'), may hold values from -0.001953125 to 0.001953125
- stats_old: float32 [4, 1, 64, 160, 640], P('mp', None, 'dp'), may hold values from -1 to 1, as said below
- owner_map: int32 [8], replicated, may hold values from 0 to 7, each once
- rotation: int32 [1], replicated, may hold values from 0 to 7
Outputs:
- update: bfloat16 [8, 2560, 640], P('mp')
- stats_new: float32 [4, 1, 64, 160, 640], P('mp', None, 'dp')
- roots_new: float32 [4, 1, 64, 160, 640], P('mp', None, 'dp')
Inputs may be any that keep to these rules, and one draw needn't show every extreme that they name: `stats_old`: each of the 4 x 8 x 2 matrices read by the reshape to [4, 8, 2, 640, 640] is symmetric positive definite. `owner_map`: a permutation of the 8 positions.
All inputs are finite; a program needn't handle non-finite values.
Results may differ from a plain program's by a relative error of at most 0.0053.
Values may be sent and summed in bfloat16 or wider, within the bound.
A program may use at most 192 MiB of HBM per device.

v0:
```python
import jax
import jax.numpy as jnp
from jax import lax
from jax.sharding import PartitionSpec as P

ITERS = 4


BETA = 0.9


def partner_2(value, axis, apart):
    mask = 2**apart
    pairs = [(source, source ^ mask) for source in range(lax.axis_size(axis))]
    return lax.ppermute(value, axis, pairs)


def shifted(block, axis, distance):
    devices = range(lax.axis_size(axis))
    route = [((i - distance) % len(devices), i) for i in devices]
    return lax.ppermute(block, axis, route)


def matmul_f32(left_op, right_op):
    return jnp.einsum("kij,kjl->kil", left_op, right_op, precision=lax.Precision.HIGHEST)


def attach(pieces, partner, bit_pos):
    lower_half = lax.axis_index("dp") >> bit_pos & 1 == 0
    return jnp.where(
        lower_half,
        jnp.concatenate([pieces, partner], axis=1),
        jnp.concatenate([partner, pieces], axis=1),
    )


def join_quad(pieces):
    for bit_pos in range(2):
        pieces = attach(
            pieces,
            partner_2(pieces.astype(jnp.bfloat16), "dp", bit_pos).astype(pieces.dtype),
            bit_pos,
        )
    return pieces


def join_grad(pieces):
    for bit_pos in range(3):
        pieces = attach(pieces, partner_2(pieces, "dp", bit_pos), bit_pos)
    return pieces


def join_roots(pieces):
    for bit_pos in range(3):
        pieces = attach(pieces, partner_2(pieces, "dp", bit_pos), bit_pos)
    return pieces


def rotate(payload, amount, block_count):
    here_group = lax.axis_index("dp") // 8
    for bit_pos in range(block_count.bit_length() - 1):
        step_size = 1 << bit_pos
        moved = shifted(payload, "dp", 8 * step_size)
        moved = jnp.where(here_group < step_size, jnp.roll(moved, 1, axis=0), moved)
        payload = jnp.where(amount >> bit_pos & 1 == 1, moved, payload)
    return payload


def newton_whole(statistic):
    identity = jnp.eye(statistic.shape[-1], dtype=jnp.float32)
    frobenius = jnp.sqrt(jnp.sum(statistic * statistic, axis=(1, 2)))
    scale = 2.5 / frobenius
    moment = scale[:, None, None] * statistic
    iterate = jnp.power(scale, 0.25)[:, None, None] * identity
    for iteration in range(ITERS):
        factor = (5.0 * identity - moment) * 0.25
        iterate = matmul_f32(iterate, factor)
        if iteration + 1 < ITERS:
            square = matmul_f32(factor, factor)
            fourth = matmul_f32(square, square)
            moment = matmul_f32(fourth, moment)
    return iterate


def local(activations, grad_out, stats_old, owner_map, rotation):
    gathered = lax.all_gather(activations, "mp", axis=1, tiled=True)
    block_size = stats_old.shape[-1]
    quarter_rows = stats_old.shape[-2]
    eighth_rows = block_size // 8
    slot_count = stats_old.shape[1]
    block_count = owner_map.shape[0]
    devices = lax.axis_size("dp")
    groups = devices // 8
    row_blocks = gathered.shape[1] // block_size
    col_blocks = grad_out.shape[1] // block_size
    dp_index = lax.axis_index("dp")
    member = dp_index % 8
    side_bit = member // 4
    quarter_index = member % 4
    places = jnp.arange(block_count, dtype=jnp.int32)
    inverse = jnp.sum(
        places[:, None] * (owner_map[:, None] == places[None, :]).astype(jnp.int32), axis=0
    )
    shift_by = rotation[0]
    pieces = slot_count * eighth_rows * lax.axis_size("dp") // eighth_rows
    piece_index = jnp.arange(pieces, dtype=jnp.int32)
    source = piece_index // slot_count
    position = piece_index % slot_count * groups + source // 8
    owned_block = jnp.sum(
        jnp.where(position[:, None] == places[None, :], inverse[None, :], 0), axis=1
    )
    row_block = owned_block % row_blocks
    col_block = owned_block // row_blocks
    columns = (row_block * block_size + source % 8 * eighth_rows)[:, None] + jnp.arange(
        eighth_rows, dtype=jnp.int32
    )[None, :]
    chosen = jnp.take(gathered, columns.reshape(-1), axis=1)
    product = lax.dot_general(
        chosen, grad_out, (((0,), (0,)), ((), ())), preferred_element_type=jnp.float32
    )
    product = product.reshape(pieces, eighth_rows, col_blocks, block_size)
    col_pick = (col_block[:, None] == jnp.arange(col_blocks, dtype=jnp.int32)[None, :]).astype(
        jnp.float32
    )
    summed = lax.psum_scatter(
        jnp.sum(product * col_pick[:, None, :, None], axis=2).reshape(
            pieces * eighth_rows, block_size
        ),
        "dp",
        scatter_dimension=0,
        tiled=True,
    )
    grad_piece = summed.astype(jnp.bfloat16).reshape(slot_count, eighth_rows, block_size)
    full_grad = join_grad(grad_piece)
    old_stats = stats_old.reshape(slot_count, quarter_rows, block_size)
    flipped = jnp.swapaxes(full_grad, 1, 2)
    oriented = jnp.where(side_bit == 0, full_grad, flipped)
    own_rows = lax.dynamic_slice_in_dim(oriented, quarter_index * quarter_rows, quarter_rows, 1)
    outer = jnp.einsum("sqc,src->sqr", own_rows, oriented, preferred_element_type=jnp.float32)
    fresh = BETA * old_stats + (1.0 - BETA) * outer
    stats_new = fresh.reshape(stats_old.shape)
    at_root = rotate(fresh, shift_by, block_count)
    statistic = join_quad(at_root)
    root_rows = lax.dynamic_slice_in_dim(
        newton_whole(statistic), quarter_index * quarter_rows, quarter_rows, 1
    )
    roots_new = root_rows.reshape(stats_old.shape)
    returned = rotate(root_rows, (block_count - shift_by) % block_count, block_count)
    both_roots = join_roots(returned)
    left_root = both_roots[:, :block_size]
    right_root = both_roots[:, block_size:]
    left_rows = lax.dynamic_slice_in_dim(left_root, member * eighth_rows, eighth_rows, 1)
    partial_rows = matmul_f32(left_rows, full_grad.astype(jnp.float32))
    precond = matmul_f32(partial_rows, right_root).astype(jnp.bfloat16)
    collected = lax.all_gather(precond, "dp", axis=1, tiled=True)
    by_place = collected.reshape(block_count, block_size, block_size)
    ordered = jnp.take(by_place, owner_map, axis=0)
    update = ordered.reshape(col_blocks, row_blocks * block_size, block_size)
    return (update, stats_new, roots_new)


def solution(mesh):
    return jax.shard_map(
        local,
        mesh=mesh,
        in_specs=(P("dp", "mp"), P("dp", "mp"), P("mp", None, "dp", None, None), P(), P()),
        out_specs=(
            P("mp", None, None),
            P("mp", None, "dp", None, None),
            P("mp", None, "dp", None, None),
        ),
        check_vma=False,
    )
```

profile of v0, /device:TPU:4, one launch (start us, length us, event | category | flops | bytes accessed | tf_op | source)
XLA Modules:
  0.0 1169.8 jit_solution(17328114603977087379)
XLA Ops:
  7.2 1.9 copy.12
  10.5 25.0 %all-gather.4.cloned.1.call-done = bf16[256,2560]{0,1:T(8,128)(2,1)} async-done(((bf16[256,640]{0,1:T(8,128)(2,1)}), bf16[256,2560]{0,1:T(8,128)(2,1)}) %all-gather.4.cloned.1.call-update) | async-done | bytes 1310736 | tf_op jit(solution)/shard_map/all_gather | solution.py:86
  35.5 17.7 %gather_fusion = bf16[5120,256]{1,0:T(8,128)(2,1)S(1)} fusion(bf16[256,2560]{0,1:T(8,128)(2,1)} %all-gather.4.cloned.1.call-done, s32[5120]{0:T(1024)S(1)} %broadcast_clamp_fusion), kind=kCustom, calls=%fused_computation | custom fusion | bytes 5263360 | tf_op jit(solution)/shard_map/jit(_take)/gather | solution.py:117
  53.1 11.5 fusion
  64.6 31.7 %reshape.1101 = f32[64,80,2,640]{3,2,1,0:T(2,128)} reshape(f32[5120,1280]{1,0:T(8,128)} %fusion) | data formatting | bytes 52428800 | tf_op jit(solution)/shard_map/reshape | solution.py:121
  96.3 127.9 %multiply_reduce_fusion = f32[64,80,640]{2,1,0:T(8,128)} fusion(f32[64,80,2,640]{3,2,1,0:T(2,128)} %reshape.1101, f32[64,2]{1,0:T(8,128)S(1)} %fusion.69), kind=kLoop, calls=%fused_computation.2 | loop fusion | flops 9830400 | bytes 39322112 | tf_op jit(solution)/shard_map/reduce_sum | solution.py:126
  224.3 353.6 %reduce-scatter.2.cloned.1.call-done = f32[80,640]{1,0:T(8,128)} async-done(((f32[5120,640]{1,0:T(8,128)}), f32[80,640]{1,0:T(8,128)}) %reduce-scatter.2.cloned.1.call-update) | async-done | bytes 204816 | tf_op jit(solution)/shard_map/reduce_scatter | solution.py:125
  577.9 0.9 convert_bitcast_fusion.2
  579.0 4.6 collective-permute-done
  583.8 0.9 convert_element_type.42
  584.8 13.1 %collective-permute-done.1 = bf16[1,160,640]{2,1,0:T(8,128)(2,1)S(1)} collective-permute-done((bf16[1,160,640]{2,1,0:T(8,128)(2,1)S(1)}, bf16[1,160,640]{2,1,0:T(8,128)(2,1)S(1)}, u32[]{:S(2)}, u32[]{:S(2)}) %collective-permute-start.1) | collective-permute-done | bytes 204832 | tf_op jit(solution)/shard_map/ppermute | solution.py:15
  598.7 13.2 %collective-permute-done.2 = bf16[1,320,640]{2,1,0:T(8,128)(2,1)S(1)} collective-permute-done((bf16[1,320,640]{2,1,0:T(8,128)(2,1)S(1)}, bf16[1,320,640]{2,1,0:T(8,128)(2,1)S(1)}, u32[]{:S(2)}, u32[]{:S(2)}) %collective-permute-start.2) | collective-permute-done | bytes 409632 | tf_op jit(solution)/shard_map/ppermute | solution.py:15
  613.0 0.9 copy.13
  614.1 0.9 copy-done.9
  616.1 9.4 collective-permute-done.3
  625.7 10.3 collective-permute-done.4
  636.2 7.9 collective-permute-done.5
  644.3 5.7 collective-permute-done.6
  650.5 12.3 %collective-permute-done.7 = bf16[1,320,640]{2,1,0:T(8,128)(2,1)S(1)} collective-permute-done((bf16[1,320,640]{2,1,0:T(8,128)(2,1)S(1)}, bf16[1,320,640]{2,1,0:T(8,128)(2,1)S(1)}, u32[]{:S(2)}, u32[]{:S(2)}) %collective-permute-start.7) | collective-permute-done | bytes 409632 | tf_op jit(solution)/shard_map/ppermute | solution.py:15
  663.0 1.0 fusion.11
  664.7 4.9 fusion.25
  669.6 4.7 fusion.102
  674.3 4.9 fusion.66
  679.2 4.7 fusion.21
  683.9 4.7 fusion.103
  688.6 4.8 fusion.104
  693.4 4.7 fusion.17
  698.1 4.7 fusion.105
  702.8 6.2 fusion.106
  709.0 6.1 fusion.14
  715.2 4.9 fusion.23
  720.1 4.7 fusion.19
  724.9 4.7 fusion.7
  730.4 10.1 collective-permute-done.8
  740.6 10.3 collective-permute-done.9
  751.1 7.9 collective-permute-done.10
  759.4 12.7 %collective-permute-done.11 = f32[1,160,640]{2,1,0:T(8,128)S(1)} collective-permute-done((f32[1,160,640]{2,1,0:T(8,128)S(1)}, f32[1,160,640]{2,1,0:T(8,128)S(1)}, u32[]{:S(2)}, u32[]{:S(2)}) %collective-permute-start.11) | collective-permute-done | bytes 409632 | tf_op jit(solution)/shard_map/ppermute | solution.py:15
  772.2 1.5 collective-permute-start.12
  773.7 20.6 %collective-permute-done.12 = f32[1,320,640]{2,1,0:T(8,128)S(1)} collective-permute-done((f32[1,320,640]{2,1,0:T(8,128)S(1)}, f32[1,320,640]{2,1,0:T(8,128)S(1)}, u32[]{:S(2)}, u32[]{:S(2)}) %collective-permute-start.12) | collective-permute-done | bytes 819232 | tf_op jit(solution)/shard_map/ppermute | solution.py:15
  794.3 1.3 maximum_select_fusion.4
  795.6 2.9 collective-permute-start.13
  798.6 39.4 %collective-permute-done.13 = f32[1,640,640]{2,1,0:T(8,128)} collective-permute-done((f32[1,640,640]{2,1,0:T(8,128)}, f32[1,640,640]{2,1,0:T(8,128)}, u32[]{:S(2)}, u32[]{:S(2)}) %collective-permute-start.13) | collective-permute-done | bytes 1638432 | tf_op jit(solution)/shard_map/ppermute | solution.py:15
  838.0 2.3 maximum_select_fusion
  840.4 0.9 copy-done.7
  842.1 1.7 fusion.29
  844.1 304.7 %all-gather.6.cloned.1.call-done = bf16[5120,640]{1,0:T(8,128)(2,1)} async-done(((bf16[80,640]{1,0:T(8,128)(2,1)}), bf16[5120,640]{1,0:T(8,128)(2,1)}) %all-gather.6.cloned.1.call-update) | async-done | bytes 6553616 | tf_op jit(solution)/shard_map/all_gather | solution.py:155
  1148.7 7.0 gather_fusion.1
  1155.7 7.3 bitcast_select_fusion
  (82 shorter events, 7.9 us)
Async XLA Ops:
  7.2 46.0 %copy-start = (bf16[256,1280]{1,0:T(8,128)(2,1)S(1)}, bf16[256,1280]{1,0:T(8,128)(2,1)}, u32[]{:S(2)}) copy-start(bf16[256,1280]{1,0:T(8,128)(2,1)} %param.6) | copy-start | bytes 1966084
  7.2 28.3 %all-gather.4.cloned.1.call-start = ((), (), s32[]{:S(2)}) async-start(), calls=%async_computation.1 | async-start | bytes 1638400 | tf_op jit(solution)/shard_map/all_gather | solution.py:86
  9.2 568.7 %reduce-scatter.2.cloned.1.call-start = ((), (), s32[]{:S(2)}) async-start(), calls=%async_computation.2 | async-start | bytes 13312000 | tf_op jit(solution)/shard_map/reduce_scatter | solution.py:125
  224.3 924.4 %all-gather.6.cloned.1.call-start = ((), (), s32[]{:S(2)}) async-start(), calls=%async_computation.3 | async-start | bytes 6656000 | tf_op jit(solution)/shard_map/all_gather | solution.py:155
  578.9 4.7 collective-permute-start
  583.7 14.2 %collective-permute-start.1 = (bf16[1,160,640]{2,1,0:T(8,128)(2,1)S(1)}, bf16[1,160,640]{2,1,0:T(8,128)(2,1)S(1)}, u32[]{:S(2)}, u32[]{:S(2)}) collective-permute-start(bf16[1,160,640]{2,1,0:T(8,128)(2,1)S(1)} %maximum_select_fusion.15), channel_id=1, source_target_pairs={{0,8},{4,12},{8,0},{12,4},{16,24},{20,28},{24,16},{28,20},{32,40},... | collective-permute-start | bytes 614408 | tf_op jit(solution)/shard_map/ppermute | solution.py:15
  598.0 13.9 %collective-permute-start.2 = (bf16[1,320,640]{2,1,0:T(8,128)(2,1)S(1)}, bf16[1,320,640]{2,1,0:T(8,128)(2,1)S(1)}, u32[]{:S(2)}, u32[]{:S(2)}) collective-permute-start(bf16[1,320,640]{2,1,0:T(8,128)(2,1)S(1)} %maximum_select_fusion.13), channel_id=1, source_target_pairs={{0,16},{4,20},{8,24},{12,28},{16,0},{20,4},{24,8},{28,12},{32,48},... | collective-permute-start | bytes 1228808 | tf_op jit(solution)/shard_map/ppermute | solution.py:15
  598.7 15.2 %copy-start.6 = (bf16[320,640]{1,0:T(8,128)(2,1)}, bf16[320,640]{1,0:T(8,128)(2,1)S(1)}, u32[]{:S(2)}) copy-start(bf16[320,640]{1,0:T(8,128)(2,1)S(1)} %maximum_select_fusion.12) | copy-start | bytes 1228804
  611.9 0.8 copy-start.10
  614.0 1.0 copy-start.9
  615.4 28.8 %copy-start.5 = (f32[160,640]{1,0:T(8,128)}, f32[160,640]{1,0:T(8,128)S(1)}, u32[]{:S(2)}) copy-start(f32[160,640]{1,0:T(8,128)S(1)} %fusion.28) | copy-start | bytes 1228804
  615.4 10.1 collective-permute-start.3
  625.6 10.4 collective-permute-start.4
  636.0 8.0 collective-permute-start.5
  644.2 5.8 collective-permute-start.6
  650.1 12.8 %collective-permute-start.7 = (bf16[1,320,640]{2,1,0:T(8,128)(2,1)S(1)}, bf16[1,320,640]{2,1,0:T(8,128)(2,1)S(1)}, u32[]{:S(2)}, u32[]{:S(2)}) collective-permute-start(bf16[1,320,640]{2,1,0:T(8,128)(2,1)S(1)} %fusion.30), channel_id=1, source_target_pairs={{0,8},{4,12},{8,0},{12,4},{16,24},{20,28},{24,16},{28,20},{32,40},... | collective-permute-start | bytes 1228808 | tf_op jit(solution)/shard_map/ppermute | solution.py:15
  663.0 11.3 copy-start.8
  679.2 9.4 copy-start.2
  709.0 6.2 copy-start.3
  720.1 4.7 copy-start.4
  730.4 10.1 collective-permute-start.8
  740.5 10.4 collective-permute-start.9
  751.0 8.0 collective-permute-start.10
  759.1 13.0 %collective-permute-start.11 = (f32[1,160,640]{2,1,0:T(8,128)S(1)}, f32[1,160,640]{2,1,0:T(8,128)S(1)}, u32[]{:S(2)}, u32[]{:S(2)}) collective-permute-start(f32[1,160,640]{2,1,0:T(8,128)S(1)} %broadcast_select_fusion.5), channel_id=1, source_target_pairs={{0,4},{4,0},{8,12},{12,8},{16,20},{20,16},{24,28},{28,24},{32,36},... | collective-permute-start | bytes 1228808 | tf_op jit(solution)/shard_map/ppermute | solution.py:15
  772.2 22.1 %collective-permute-start.12 = (f32[1,320,640]{2,1,0:T(8,128)S(1)}, f32[1,320,640]{2,1,0:T(8,128)S(1)}, u32[]{:S(2)}, u32[]{:S(2)}) collective-permute-start(f32[1,320,640]{2,1,0:T(8,128)S(1)} %maximum_select_fusion.9), channel_id=1, source_target_pairs={{0,8},{4,12},{8,0},{12,4},{16,24},{20,28},{24,16},{28,20},{32,40},... | collective-permute-start | bytes 2457608 | tf_op jit(solution)/shard_map/ppermute | solution.py:15
  795.6 42.5 %collective-permute-start.13 = (f32[1,640,640]{2,1,0:T(8,128)}, f32[1,640,640]{2,1,0:T(8,128)}, u32[]{:S(2)}, u32[]{:S(2)}) collective-permute-start(f32[1,640,640]{2,1,0:T(8,128)} %maximum_select_fusion.4), channel_id=1, source_target_pairs={{0,16},{4,20},{8,24},{12,28},{16,0},{20,4},{24,8},{28,12},{32,48},... | collective-permute-start | bytes 4915208 | tf_op jit(solution)/shard_map/ppermute | solution.py:15
  840.3 1.0 copy-start.7
  840.3 1.1 copy-start.11
  842.1 1.8 copy-start.12
  1155.7 7.3 copy-start.1
Sparse Core Ops, SparseCore 0:
  10.4 25.0 all-gather.3
  224.4 353.4 reduce-scatter.1
  843.9 304.7 all-gather.5
where the time goes:
time: 1180 us; the launch traced here: 1170 us
  waiting for transfers between devices  861 us (73%)
  other arithmetic  144 us (12%)
  matrix products  78.9 us (7%)
  local copies, waits for them, and re-layouts  63.2 us (5%)
  between operations  16 us (1%)
    reduce_scatter x1, waiting for transfers between devices, local(): lax.psum_scatter(jnp.sum(product * col_pick[:, None, :, None], axis=2).re...  354 us
    all_gather x1, waiting for transfers between devices, local(): collected = lax.all_gather(precond, 'dp', axis=1, tiled=True)  305 us
    reduce_sum x1, other arithmetic, local(): jnp.sum(product * col_pick[:, None, :, None], axis=2)  128 us
    ppermute x8, waiting for transfers between devices, partner_2(): return lax.ppermute(value, axis, pairs)  122 us
    dot_general x15, matrix products, matmul_f32(): jnp.einsum('kij,kjl->kil', left_op, right_op, precision=lax.Precision.HIG...  67.1 us
    ppermute x6, waiting for transfers between devices, shifted(): return lax.ppermute(block, axis, route)  56 us
    reshape x1, local copies, waits for them, and re-layouts, local(): product = product.reshape(pieces, eighth_rows, col_blocks, block_size)  31.7 us
    all_gather x1, waiting for transfers between devices, local(): gathered = lax.all_gather(activations, 'mp', axis=1, tiled=True)  25 us
  transfers between devices with their start and end apart: 17, of which 17 were waited for; matrix products, arithmetic and copies ran while one was open for 0% of the time, Pallas kernels for 0%

commit v1 on v0

v1 whole, which is shorter than its diff:
```python
import jax
import jax.numpy as jnp
from jax import lax
from jax.experimental import pallas as pl
from jax.experimental.pallas import tpu as pltpu
from jax.sharding import PartitionSpec as P

BETA = 0.9
MESH = pl.DeviceIdType.MESH
VMEM = pl.BlockSpec(memory_space=pltpu.VMEM)
SMEM = pl.BlockSpec(memory_space=pltpu.SMEM)
F32 = jnp.float32
BF16 = jnp.bfloat16


def place():
    dp = lax.axis_index("dp")
    mp = lax.axis_index("mp")
    return dp // 32, lax.rem(dp // 8, 4), lax.rem(dp, 8), mp // 2, lax.rem(mp, 2)


def device(x_lo, y, z, x_hi, core):
    return {"dp": x_lo * 32 + y * 8 + z, "mp": x_hi * 2 + core}


def greet(peers):
    barrier = pltpu.get_barrier_semaphore()
    for peer in peers:
        pl.semaphore_signal(barrier, inc=1, device_id=peer, device_id_type=MESH)
    pl.semaphore_wait(barrier, len(peers))


def remote(src, dst, send, recv, peer):
    return pltpu.make_async_remote_copy(
        src_ref=src, dst_ref=dst, send_sem=send, recv_sem=recv, device_id=peer, device_id_type=MESH
    )


class Ring:
    def __init__(self, slot, send, recv, peers, z):
        self.slot, self.send, self.recv = slot, send, recv
        self.up, self.down = peers
        self.z = z

    def copy_up(self, step):
        i = lax.rem(self.z - step + 8, 8)
        return remote(self.slot(i), self.slot(i), self.send.at[step], self.recv.at[step], self.up)

    def copy_down(self, step):
        i = lax.rem(self.z + step, 8)
        return remote(
            self.slot(i), self.slot(i), self.send.at[4 + step], self.recv.at[4 + step], self.down
        )

    def start(self, step):
        self.copy_up(step).start()
        if step < 3:
            self.copy_down(step).start()

    def arrived(self, step):
        self.copy_up(step).wait_recv()
        if step < 3:
            self.copy_down(step).wait_recv()

    def drain(self):
        for step in range(4):
            self.copy_up(step).wait_send()
            if step < 3:
                self.copy_down(step).wait_send()


def gather_kernel(
    act_ref, gout_ref, stat_ref, owner_ref, grad_ref, stats_ref,
    actg, goutg, total, part, rsbuf, gbuf,
    x_sem, a1_sem, a2_send, a_recv, g_send, g_recv, f_send, f_recv,
    st_send, st_recv, rs_send, rs_recv, gg_send, gg_recv, zz_send, zz_recv, loc_sem,
):
    x_lo, y, z, x_hi, core = place()
    mp = x_hi * 2 + core
    group = x_lo * 4 + y
    y_up, y_down, y_far = lax.rem(y + 1, 4), lax.rem(y + 3, 4), lax.rem(y + 2, 4)
    other_x = 1 - x_lo
    partner = device(other_x, y, z, x_hi, core)
    outer = device(other_x, y, z, 1 - x_hi, core)
    twin = device(x_lo, y, z, x_hi, 1 - core)
    z_peer = [device(x_lo, y, lax.rem(z + k, 8), x_hi, core) for k in range(1, 8)]
    up_y = device(x_lo, y_up, z, x_hi, core)
    down_y = device(x_lo, y_down, z, x_hi, core)
    g_peer = []
    for k in range(1, 8):
        g = lax.rem(group + k, 8)
        g_peer.append(device(g // 4, lax.rem(g, 4), z, x_hi, core))
    greet(z_peer + g_peer + [outer, twin])

    same = core == lax.rem(y, 2)
    root = jnp.logical_and(same, x_hi == y // 2)
    mid = jnp.logical_and(same, x_hi != y // 2)
    stray = y != mp

    half = gout_ref.at[:, pl.ds(pl.multiple_of(x_lo * 640, 128), 640)]
    away = gout_ref.at[:, pl.ds(pl.multiple_of(other_x * 640, 128), 640)]
    x_copy = remote(away, goutg.at[group], x_sem.at[0], x_sem.at[1], partner)
    x_copy.start()
    a1_copy = remote(
        act_ref, actg.at[group], a1_sem, a_recv.at[group], device(x_lo, mp, z, x_hi, core)
    )

    @pl.when(stray)
    def _():
        a1_copy.start()

    own_up = remote(half, goutg.at[group], g_send.at[0], g_recv.at[0], up_y)
    own_down = remote(half, goutg.at[group], g_send.at[1], g_recv.at[1], down_y)
    own_up.start()
    own_down.start()
    keep = pltpu.make_async_copy(half, goutg.at[group], loc_sem.at[0])
    keep.start()
    mine = pltpu.make_async_copy(act_ref, actg.at[group], loc_sem.at[1])

    @pl.when(jnp.logical_not(stray))
    def _():
        mine.start()

    stats_ref[z] = stat_ref[...]
    stats = Ring(lambda i: stats_ref.at[i], st_send, st_recv, (z_peer[0], z_peer[6]), z)
    stats.start(0)

    first = jnp.where(root, x_lo, other_x)

    def a_landed(slot):
        remote(actg.at[slot], actg.at[slot], a1_sem, a_recv.at[slot], partner).wait_recv()

    def a_send(slot, index, peer):
        return remote(actg.at[slot], actg.at[slot], a2_send.at[index], a_recv.at[slot], peer)

    def from_root():
        for k in range(4):
            slot = x_lo * 4 + k

            @pl.when(y == k)
            def _():
                mine.wait()

            @pl.when(y != k)
            def _():
                a_landed(slot)

            a_send(slot, k, partner).start()
            a_send(slot, 12 + k, outer).start()
            a_send(slot, 4 + k, twin).start()

    def from_mid(ks):
        for k in ks:
            slot = other_x * 4 + k
            a_landed(slot)
            a_send(slot, k, partner).start()
            a_send(slot, 4 + k, twin).start()

    stats.arrived(0)
    stats.start(1)
    pl.when(root)(from_root)

    pair_slot = other_x * 4 + y
    remote(goutg.at[pair_slot], goutg.at[pair_slot], x_sem.at[0], x_sem.at[1], partner).wait_recv()
    pair_up = remote(goutg.at[pair_slot], goutg.at[pair_slot], g_send.at[2], g_recv.at[2], up_y)
    pair_down = remote(goutg.at[pair_slot], goutg.at[pair_slot], g_send.at[3], g_recv.at[3], down_y)
    pair_up.start()
    pair_down.start()
    stats.arrived(1)
    stats.start(2)
    pl.when(mid)(lambda: from_mid((0, 1)))

    def along_y(column, index):
        low = column * 4 + y_down
        high = column * 4 + y_up
        remote(goutg.at[low], goutg.at[low], g_send.at[index], g_recv.at[index], up_y).wait_recv()
        on_up = remote(
            goutg.at[low, pl.ds(0, 128)], goutg.at[low, pl.ds(0, 128)],
            f_send.at[index], f_recv.at[index], up_y,
        )
        on_up.start()
        remote(
            goutg.at[high], goutg.at[high], g_send.at[index + 1], g_recv.at[index + 1], down_y
        ).wait_recv()
        on_down = remote(
            goutg.at[high, pl.ds(128, 128)], goutg.at[high, pl.ds(128, 128)],
            f_send.at[index + 1], f_recv.at[index + 1], down_y,
        )
        on_down.start()
        return [on_up, on_down]

    passed = along_y(x_lo, 0)
    stats.arrived(2)
    stats.start(3)
    pl.when(mid)(lambda: from_mid((2, 3)))
    passed += along_y(other_x, 2)
    stats.arrived(3)

    def to_twin():
        for k in range(4):
            slot = (1 - first) * 4 + k
            a_landed(slot)
            a_send(slot, 8 + k, twin).start()

    pl.when(same)(to_twin)

    @pl.when(jnp.logical_not(same))
    def _():
        for slot in range(8):
            a_landed(slot)

    for copy in passed:
        copy.wait_recv()
    keep.wait()

    def multiply(step):
        left = actg[pl.ds(step * 2, 2)].reshape(512, 640)
        right = goutg[pl.ds(step * 2, 2)].reshape(512, 640)
        return lax.dot_general(left, right, (((0,), (0,)), ((), ())), preferred_element_type=F32)

    total[...] = multiply(0)

    def accumulate(step, carry):
        total[...] += multiply(step)
        return carry

    lax.fori_loop(1, 4, accumulate, 0)
    for k in range(8):
        part[k] = total[pl.ds(k * 80, 80), :].astype(BF16)

    sums = []
    for k in range(1, 8):
        to = lax.rem(z + k, 8)
        copy = remote(part.at[to], rsbuf.at[k], rs_send.at[k], rs_recv.at[k], z_peer[k - 1])
        copy.start()
        sums.append(copy)
    rows = total[pl.ds(pl.multiple_of(z * 80, 8), 80), :]
    for k in range(1, 8):
        sums[k - 1].wait_recv()
        rows = rows + rsbuf[k].astype(F32)
    gbuf[group] = rows.astype(BF16)

    spread = []
    for k in range(1, 8):
        copy = remote(gbuf.at[group], gbuf.at[group], gg_send.at[k], gg_recv.at[k], g_peer[k - 1])
        copy.start()
        spread.append(copy)
    block = jnp.int32(0)
    for b in range(8):
        block = jnp.where(owner_ref[b] == group, b, block)
    for copy in spread:
        copy.wait_recv()
    grad_ref[z] = gbuf[block]
    ring = Ring(lambda i: grad_ref.at[i], zz_send, zz_recv, (z_peer[0], z_peer[6]), z)
    for step in range(4):
        ring.start(step)
        ring.arrived(step)

    ring.drain()
    stats.drain()
    for copy in spread + sums + passed + [x_copy, own_up, own_down, pair_up, pair_down]:
        copy.wait_send()

    @pl.when(stray)
    def _():
        a1_copy.wait_send()

    @pl.when(same)
    def _():
        for k in range(4):
            a_send(k, k, partner).wait_send()
            a_send(k, 4 + k, twin).wait_send()
            a_send(k, 8 + k, twin).wait_send()

    @pl.when(root)
    def _():
        for k in range(4):
            a_send(k, 12 + k, outer).wait_send()


def gather_gradient(activations, grad_out, stat_rows, owner_map):
    dma = pltpu.SemaphoreType.DMA
    return pl.pallas_call(
        gather_kernel,
        out_shape=(
            jax.ShapeDtypeStruct((8, 80, 640), BF16),
            jax.ShapeDtypeStruct((8, 160, 640), BF16),
        ),
        in_specs=[VMEM, VMEM, VMEM, SMEM],
        out_specs=(VMEM, VMEM),
        scratch_shapes=[
            pltpu.VMEM((8, 256, 640), BF16),
            pltpu.VMEM((8, 256, 640), BF16),
            pltpu.VMEM((640, 640), F32),
            pltpu.VMEM((8, 80, 640), BF16),
            pltpu.VMEM((8, 80, 640), BF16),
            pltpu.VMEM((8, 80, 640), BF16),
            dma((2,)), dma, dma((16,)), dma((8,)), dma((4,)), dma((4,)), dma((4,)), dma((4,)),
            dma((7,)), dma((7,)), dma((8,)), dma((8,)), dma((8,)), dma((8,)), dma((7,)), dma((7,)),
            dma((2,)),
        ],
        compiler_params=pltpu.CompilerParams(
            collective_id=0, has_side_effects=True, vmem_limit_bytes=48 * 2**20
        ),
        name="gather_gradient",
    )(activations, grad_out, stat_rows, owner_map)


def dot(a, b):
    return jnp.dot(a, b, preferred_element_type=F32)


def root_kernel(
    grad_ref, stats_ref, old_ref, stats_out, roots_out, update_out,
    both, moment, wide, low1, low2, low3, low_w, scales,
):
    z = lax.rem(lax.axis_index("dp"), 8)
    side = z // 4
    quarter = pl.multiple_of(lax.rem(z, 4) * 160, 16)
    eighth = pl.multiple_of(z * 80, 16)
    both[0] = grad_ref[...]
    both[1] = grad_ref[...].astype(F32).T.astype(BF16)

    own = dot(both[side, pl.ds(quarter, 160), :], both[1 - side])
    stats_out[...] = BETA * old_ref[...] + (1.0 - BETA) * own

    def start(s, carry):
        a = BETA * stats_ref[s].astype(F32) + (1.0 - BETA) * dot(both[s], both[1 - s])
        moment[s] = a
        norm = jnp.sqrt(jnp.sum(a * a, keepdims=True))
        scale = 2.5 / norm
        scales[s] = jnp.broadcast_to(jnp.sqrt(jnp.sqrt(scale)), (8, 128))
        m = moment[s] * scale
        moment[s] = m
        low1[s] = m.astype(BF16)
        return carry

    lax.fori_loop(0, 2, start, 0)

    def advance(now, later):
        def square(s, carry):
            w = dot(now[s], now[s]) - 10.0 * moment[s]
            wide[s] = w
            low_w[s] = w.astype(BF16)
            return carry

        def fourth(s, carry):
            h = dot(low_w[s], low_w[s]) + 50.0 * wide[s]
            wide[s] = h
            return carry

        def finish(s, carry):
            m = (625.0 * moment[s] + dot(now[s], wide[s].astype(BF16))) * (1.0 / 256.0)
            moment[s] = m
            later[s] = m.astype(BF16)
            return carry

        lax.fori_loop(0, 2, square, 0)
        lax.fori_loop(0, 2, fourth, 0)
        lax.fori_loop(0, 2, finish, 0)

    advance(low1, low2)
    advance(low2, low3)

    def factor(r, low, s):
        return 1.25 * r - 0.25 * dot(r.astype(BF16), low[s])

    def chain(r, s):
        r = factor(r, low2, s)
        r = factor(r, low3, s)
        t = r
        for _ in range(4):
            t = factor(t, low3, s)
        return 1.25 * r - 0.25 * dot(t.astype(BF16), low3[s])

    def identity(rows, offset):
        across = lax.broadcasted_iota(jnp.int32, (rows, 640), 1)
        down = lax.broadcasted_iota(jnp.int32, (rows, 640), 0) + offset
        return (across == down).astype(F32)

    def first(rows, offset, s):
        m = low1[s, pl.ds(offset, rows), :].astype(F32)
        return (1.25 * identity(rows, offset) - 0.25 * m) * scales[s, 0:1, 0:1]

    roots_out[...] = chain(first(160, quarter, side), side).astype(BF16)
    left = chain(first(80, eighth, 0), 0)
    high = left.astype(BF16)
    low = (left - high.astype(F32)).astype(BF16)
    y = dot(high, both[0]) + dot(low, both[0])
    y = factor(y, low1, 1) * scales[1, 0:1, 0:1]
    update_out[...] = chain(y, 1).astype(BF16)


def compute_roots(grad, stats, old_rows):
    return pl.pallas_call(
        root_kernel,
        out_shape=(
            jax.ShapeDtypeStruct((160, 640), F32),
            jax.ShapeDtypeStruct((160, 640), BF16),
            jax.ShapeDtypeStruct((80, 640), BF16),
        ),
        in_specs=[VMEM, VMEM, VMEM],
        out_specs=(VMEM, VMEM, VMEM),
        scratch_shapes=[
            pltpu.VMEM((2, 640, 640), BF16),
            pltpu.VMEM((2, 640, 640), F32),
            pltpu.VMEM((2, 640, 640), F32),
            pltpu.VMEM((2, 640, 640), BF16),
            pltpu.VMEM((2, 640, 640), BF16),
            pltpu.VMEM((2, 640, 640), BF16),
            pltpu.VMEM((2, 640, 640), BF16),
            pltpu.VMEM((2, 8, 128), F32),
        ],
        compiler_params=pltpu.CompilerParams(vmem_limit_bytes=48 * 2**20),
        name="compute_roots",
    )(grad, stats, old_rows)


def spread_kernel(
    piece_ref, root_ref, rotation_ref, update_ref, roots_out, rot0, rot1, rot2,
    a_send, a_recv, az_send, az_recv, bz_send, bz_recv,
    x_send, x_recv, y_send, y_recv, f_send, f_recv, c_send, c_recv, rot_send, rot_recv,
):
    x_lo, y, z, x_hi, core = place()
    group = x_lo * 4 + y
    other_x = 1 - x_lo
    pair = other_x * 4 + y
    y_up, y_down, y_far = lax.rem(y + 1, 4), lax.rem(y + 3, 4), lax.rem(y + 2, 4)
    partner = device(other_x, y, z, x_hi, core)
    up_y = device(x_lo, y_up, z, x_hi, core)
    down_y = device(x_lo, y_down, z, x_hi, core)
    up_z = device(x_lo, y, lax.rem(z + 1, 8), x_hi, core)
    down_z = device(x_lo, y, lax.rem(z + 7, 8), x_hi, core)
    g_peer = []
    for k in range(1, 8):
        g = lax.rem(group + k, 8)
        g_peer.append(device(g // 4, lax.rem(g, 4), z, x_hi, core))
    greet(g_peer + [up_z, down_z])

    update_ref[group, z] = piece_ref[...]
    rots = (rot0, rot1, rot2)
    rot0[0] = root_ref[...]

    ring_b = Ring(
        lambda i: update_ref.at[group, i, pl.ds(32, 48)], bz_send, bz_recv, (up_z, down_z), z
    )
    ring_a = Ring(lambda i: update_ref.at[:, i, pl.ds(0, 32)], az_send, az_recv, (up_z, down_z), z)
    ring_b.start(0)
    over = []
    for k in range(1, 8):
        own = update_ref.at[group, z, pl.ds(0, 32)]
        copy = remote(own, own, a_send.at[k], a_recv.at[k], g_peer[k - 1])
        copy.start()
        over.append(copy)

    def rotate(step):
        return remote(
            rots[step].at[0], rots[step].at[1], rot_send.at[step], rot_recv.at[step],
            g_peer[(1 << step) - 1],
        )

    def rotated(step):
        rotate(step).wait_recv()
        bit = lax.rem(rotation_ref[0] // (1 << step), 2)
        return rots[step][bit]

    rotate(0).start()
    ring_b.arrived(0)
    ring_b.start(1)
    ring_b.arrived(1)
    ring_b.start(2)
    for copy in over:
        copy.wait_recv()
    ring_a.start(0)
    ring_b.arrived(2)
    ring_b.start(3)
    ring_b.arrived(3)

    def rows(g, start, count, z0=0, zs=8):
        return update_ref.at[g, pl.ds(z0, zs), pl.ds(start, count)]

    def send(ref, sems, index, peer):
        copy = remote(ref, ref, sems[0].at[index], sems[1].at[index], peer)
        copy.start()
        return copy

    def landed(ref, sems, index):
        remote(ref, ref, sems[0].at[index], sems[1].at[index], partner).wait_recv()

    ys, fs, cs, xs = (y_send, y_recv), (f_send, f_recv), (c_send, c_recv), (x_send, x_recv)
    sent = []
    sent.append(send(rows(group, 32, 48), xs, 0, partner))
    sent.append(send(rows(group, 32, 48), ys, 0, up_y))
    sent.append(send(rows(group, 32, 48), ys, 1, down_y))

    rot1[0] = rotated(0)
    rotate(1).start()
    ring_a.arrived(0)
    ring_a.start(1)

    landed(rows(pair, 32, 48), xs, 0)
    sent.append(send(rows(pair, 32, 32), ys, 2, up_y))
    sent.append(send(rows(pair, 32, 32), ys, 3, down_y))

    low, high, far = x_lo * 4 + y_down, x_lo * 4 + y_up, x_lo * 4 + y_far
    landed(rows(low, 32, 48), ys, 0)
    sent.append(send(rows(low, 32, 48, 0, 4), fs, 0, up_y))
    sent.append(send(rows(low, 64, 16), cs, 0, partner))
    landed(rows(high, 32, 48), ys, 1)
    sent.append(send(rows(high, 32, 48, 4, 4), fs, 1, down_y))
    sent.append(send(rows(high, 64, 16), cs, 1, partner))

    ring_a.arrived(1)
    ring_a.start(2)
    rot2[0] = rotated(1)
    rotate(2).start()

    p_low, p_high, p_far = other_x * 4 + y_down, other_x * 4 + y_up, other_x * 4 + y_far
    landed(rows(p_low, 32, 32), ys, 2)
    sent.append(send(rows(p_low, 32, 32, 0, 4), fs, 2, up_y))
    landed(rows(p_high, 32, 32), ys, 3)
    sent.append(send(rows(p_high, 32, 32, 4, 4), fs, 3, down_y))
    landed(rows(far, 32, 48, 0, 4), fs, 0)
    landed(rows(far, 32, 48, 4, 4), fs, 1)
    sent.append(send(rows(far, 64, 16), cs, 2, partner))

    ring_a.arrived(2)
    ring_a.start(3)
    roots_out[...] = rotated(2).astype(F32)

    landed(rows(p_low, 64, 16), cs, 0)
    landed(rows(p_high, 64, 16), cs, 1)
    landed(rows(p_far, 32, 32, 0, 4), fs, 2)
    landed(rows(p_far, 32, 32, 4, 4), fs, 3)
    landed(rows(p_far, 64, 16), cs, 2)
    ring_a.arrived(3)

    ring_a.drain()
    ring_b.drain()
    for copy in sent + over:
        copy.wait_send()
    for step in range(3):
        rotate(step).wait_send()


def spread_update(piece, root_rows, rotation):
    dma = pltpu.SemaphoreType.DMA
    return pl.pallas_call(
        spread_kernel,
        out_shape=(
            jax.ShapeDtypeStruct((8, 8, 80, 640), BF16),
            jax.ShapeDtypeStruct((160, 640), F32),
        ),
        in_specs=[VMEM, VMEM, SMEM],
        out_specs=(VMEM, VMEM),
        scratch_shapes=[
            pltpu.VMEM((2, 160, 640), BF16),
            pltpu.VMEM((2, 160, 640), BF16),
            pltpu.VMEM((2, 160, 640), BF16),
            dma((8,)), dma((8,)), dma((7,)), dma((7,)), dma((7,)), dma((7,)),
            dma((1,)), dma((1,)), dma((4,)), dma((4,)), dma((4,)), dma((4,)),
            dma((3,)), dma((3,)), dma((3,)), dma((3,)),
        ],
        compiler_params=pltpu.CompilerParams(
            collective_id=1, has_side_effects=True, vmem_limit_bytes=48 * 2**20
        ),
        name="spread_update",
    )(piece, root_rows, rotation)


def order_kernel(owner_ref, in_ref, out_ref):
    out_ref[...] = in_ref[...]


def order_blocks(by_place, owner_map):
    return pl.pallas_call(
        order_kernel,
        out_shape=jax.ShapeDtypeStruct((8, 640, 640), BF16),
        grid_spec=pltpu.PrefetchScalarGridSpec(
            num_scalar_prefetch=1,
            grid=(8,),
            in_specs=[pl.BlockSpec((1, 640, 640), lambda b, owner: (owner[b], 0, 0))],
            out_specs=pl.BlockSpec((1, 640, 640), lambda b, owner: (b, 0, 0)),
        ),
        name="order_blocks",
    )(owner_map, by_place)


def local(activations, grad_out, stats_old, owner_map, rotation):
    old_rows = stats_old.reshape(160, 640)
    grad, stats = gather_gradient(activations, grad_out, old_rows.astype(BF16), owner_map)
    stats_new, root_rows, piece = compute_roots(
        grad.reshape(640, 640), stats.reshape(2, 640, 640), old_rows
    )
    by_place, roots_new = spread_update(piece, root_rows, rotation)
    update = order_blocks(by_place.reshape(8, 640, 640), owner_map)
    return (
        update.reshape(2, 2560, 640),
        stats_new.reshape(stats_old.shape),
        roots_new.reshape(stats_old.shape),
    )


def solution(mesh):
    return jax.shard_map(
        local,
        mesh=mesh,
        in_specs=(P("dp", "mp"), P("dp", "mp"), P("mp", None, "dp", None, None), P(), P()),
        out_specs=(
            P("mp", None, None),
            P("mp", None, "dp", None, None),
            P("mp", None, "dp", None, None),
        ),
        check_vma=False,
    )
```

time: 1180 us -> 185 us (0.16)
  waiting for transfers between devices: 861 us -> 0 us
  Pallas kernels: 0 us -> 175 us
  other arithmetic: 144 us -> 1.03 us
  matrix products: 78.9 us -> 0 us
  local copies, waits for them, and re-layouts: 63.2 us -> 4.46 us
  between operations: 16 us -> 1.32 us
    reduce_scatter x1 -> x0, waiting for transfers between devices: 354 us -> none  [local(): lax.psum_scatter(jnp.sum(product * col_pick[:, None, :, None], axis=2).re...]
    all_gather x2 -> x0, waiting for transfers between devices: 330 us -> none  [the longest x1 305 us: local(): collected = lax.all_gather(precond, 'dp', axis=1, tiled=True)]
    ppermute x14 -> x0, waiting for transfers between devices: 178 us -> none  [the longest x8 122 us: partner_2(): return lax.ppermute(value, axis, pairs)]
    pallas_call x0 -> x4, Pallas kernels: none -> 175 us  [the longest x1 90.1 us: gather_gradient(): pl.pallas_call(gather_kernel, out_shape=(jax.ShapeDtypeStruct((8, 80, 640...]
    reduce_sum x4 -> x0, other arithmetic: 130 us -> none  [the longest x1 128 us: local(): jnp.sum(product * col_pick[:, None, :, None], axis=2)]
    dot_general x17 -> x0, matrix products: 78.9 us -> none  [the longest x15 67.1 us: matmul_f32(): jnp.einsum('kij,kjl->kil', left_op, right_op, precision=lax.Precision.HIG...]
    reshape x2 -> x0, local copies, waits for them, and re-layouts: 32.5 us -> none  [the longest x1 31.7 us: local(): product = product.reshape(pieces, eighth_rows, col_blocks, block_size)]
    gather x2 -> x0, local copies, waits for them, and re-layouts: 24.7 us -> none  [the longest x1 17.7 us: local(): chosen = jnp.take(gathered, columns.reshape(-1), axis=1)]
  transfers between devices with their start and end apart: 17 -> 0, of which waited for: 17 -> 0; matrix products, arithmetic and copies ran while one was open for 0% -> 0% of each run, Pallas kernels for 0% -> 0%
where the time goes in v1:
time: 185 us; the launch traced here: 181 us
  Pallas kernels  175 us (95%)
  local copies, waits for them, and re-layouts  4.46 us (2%)
    pallas_call x1, Pallas kernels, gather_gradient(): pl.pallas_call(gather_kernel, out_shape=(jax.ShapeDtypeStruct((8, 80, 640...  90.1 us
    pallas_call x1, Pallas kernels, spread_update(): pl.pallas_call(spread_kernel, out_shape=(jax.ShapeDtypeStruct((8, 8, 80,...  56.5 us
    pallas_call x1, Pallas kernels, compute_roots(): pl.pallas_call(root_kernel, out_shape=(jax.ShapeDtypeStruct((160, 640), F...  19.2 us
    pallas_call x1, Pallas kernels, order_blocks(): pl.pallas_call(order_kernel, out_shape=jax.ShapeDtypeStruct((8, 640, 640)...  8.67 us
    unnamed x9, local copies, waits for them, and re-layouts  4.46 us

profile of v1, /device:TPU:4, one launch (start us, length us, event | category | flops | bytes accessed | tf_op | source)
XLA Modules:
  0.0 181.3 jit_solution(7348419665427564542)
XLA Ops:
  1.3 1.0 bitcast_convert_fusion.stat_ref
  2.3 0.0 copy-start.1
  2.3 1.1 copy-done.1
  3.4 0.0 copy-start.2
  3.4 1.0 copy-done.2
  4.4 0.0 copy-start.3
  4.4 0.7 copy-done.3
  5.0 90.1 %gather_gradient.1 = (bf16[8,80,640]{2,1,0:T(8,128)(2,1)S(1)}, bf16[8,160,640]{2,1,0:T(8,128)(2,1)S(1)}) custom-call(bf16[256,640]{1,0:T(8,128)(2,1)S(1)} %copy-done.2, bf16[256,1280]{1,0:T(8,128)(2,1)S(1)} %copy-done.1, bf16[160,640]{1,0:T(8,128)(2,1)S(1)} %bitcast_convert_fusion.stat_ref, s32[8]{0:T(128)S(1)} %copy-done.3), custom_call_target="tpu_custom_call" | custom-call | tf_op jit(solution)/shard_map/gather_gradient/pallas_call | solution.py:283
  95.1 0.0 copy-start
  95.2 1.0 copy-done
  96.2 19.2 %compute_roots.1 = (f32[160,640]{1,0:T(8,128)}, bf16[160,640]{1,0:T(8,128)(2,1)S(1)}, bf16[80,640]{1,0:T(8,128)(2,1)S(1)}) custom-call(bf16[640,640]{1,0:T(8,128)(2,1)S(1)} %bitcast.10, bf16[2,640,640]{2,1,0:T(8,128)(2,1)S(1)} %bitcast.8, f32[160,640]{1,0:T(8,128)S(1)} %bitcast.9), custom_call_target="tpu_custom_call" | custom-call | tf_op jit(solution)/shard_map/compute_roots/pallas_call | solution.py:395
  115.4 56.5 %spread_update.1 = (bf16[8,8,80,640]{3,2,1,0:T(8,128)(2,1)}, f32[160,640]{1,0:T(8,128)S(1)}) custom-call(bf16[80,640]{1,0:T(8,128)(2,1)S(1)} %get-tuple-element.12.piece_ref, bf16[160,640]{1,0:T(8,128)(2,1)S(1)} %get-tuple-element.13.root_ref, s32[1]{0:T(128)S(6)} %copy.9.rotation_ref), custom_call_target="tpu_custom_call" | custom-call | tf_op jit(solution)/shard_map/spread_update/pallas_call | solution.py:548
  171.9 8.7 %order_blocks.1 = bf16[8,640,640]{2,1,0:T(8,128)(2,1)} custom-call(s32[8]{0:T(128)} %owner_ref.3, bf16[8,640,640]{2,1,0:T(8,128)(2,1)} %bitcast.13), custom_call_target="tpu_custom_call" | custom-call | tf_op jit(solution)/shard_map/order_blocks/pallas_call | solution.py:576
  180.6 0.8 copy.10
Async XLA Ops:
  2.3 1.1 copy-start.1
  3.4 1.0 copy-start.2
  4.4 0.7 copy-start.3
  95.1 1.0 copy-start

commit v2 on v1

v2 whole, which is shorter than its diff:
```python
import jax
import jax.numpy as jnp
from jax import lax
from jax.experimental import pallas as pl
from jax.experimental.pallas import tpu as pltpu
from jax.sharding import PartitionSpec as P

BETA = 0.9
MESH = pl.DeviceIdType.MESH
VMEM = pl.BlockSpec(memory_space=pltpu.VMEM)
SMEM = pl.BlockSpec(memory_space=pltpu.SMEM)
F32 = jnp.float32
BF16 = jnp.bfloat16


def place():
    dp = lax.axis_index("dp")
    mp = lax.axis_index("mp")
    return dp // 32, lax.rem(dp // 8, 4), lax.rem(dp, 8), mp // 2, lax.rem(mp, 2)


def device(x_lo, y, z, x_hi, core):
    return {"dp": x_lo * 32 + y * 8 + z, "mp": x_hi * 2 + core}


def remote(src, dst, send, recv, peer):
    return pltpu.make_async_remote_copy(
        src_ref=src, dst_ref=dst, send_sem=send, recv_sem=recv, device_id=peer, device_id_type=MESH
    )


class Ring:
    def __init__(self, slot, send, recv, peers, z):
        self.slot, self.send, self.recv = slot, send, recv
        self.up, self.down = peers
        self.z = z

    def copy_up(self, step):
        i = lax.rem(self.z - step + 8, 8)
        return remote(self.slot(i), self.slot(i), self.send.at[step], self.recv.at[step], self.up)

    def copy_down(self, step):
        i = lax.rem(self.z + step, 8)
        return remote(
            self.slot(i), self.slot(i), self.send.at[4 + step], self.recv.at[4 + step], self.down
        )

    def start(self, step):
        self.copy_up(step).start()
        if step < 3:
            self.copy_down(step).start()

    def arrived(self, step):
        self.copy_up(step).wait_recv()
        if step < 3:
            self.copy_down(step).wait_recv()

    def drain(self):
        for step in range(4):
            self.copy_up(step).wait_send()
            if step < 3:
                self.copy_down(step).wait_send()


def swap(v):
    return lax.rem(v, 2) * 2 + v // 2


SWAP = (0, 2, 1, 3)
CHUNKS = ((0, 384), (384, 256))
OWN, PAIR, ON_OWN, ON_PAIR = range(4)


def gather_kernel(
    act_ref, gout_ref, old_ref, owner_ref, grad_ref, stats_ref,
    act_in, act_t, old_in, actg, goutg, total0, total1, part0, part1, rs0, rs1, gg0, gg1,
    x_send, x_recv, a1_sem, a2_send, a_recv, g_send, g_recv,
    st_send, st_recv, rs_send, rs_recv, gg_send, gg_recv, z0_send, z0_recv, z1_send, z1_recv,
    loc_sem,
):
    totals, parts, rss, ggs = (total0, total1), (part0, part1), (rs0, rs1), (gg0, gg1)
    x_lo, y, z, x_hi, core = place()
    mp = x_hi * 2 + core
    group = x_lo * 4 + y
    y_up, y_down, y_far = lax.rem(y + 1, 4), lax.rem(y + 3, 4), lax.rem(y + 2, 4)
    other_x = 1 - x_lo
    partner = device(other_x, y, z, x_hi, core)
    outer = device(other_x, y, z, 1 - x_hi, core)
    twin = device(x_lo, y, z, x_hi, 1 - core)
    z_peer = [device(x_lo, y, lax.rem(z + k, 8), x_hi, core) for k in range(1, 8)]
    y_peer = (device(x_lo, y_up, z, x_hi, core), device(x_lo, y_down, z, x_hi, core))
    g_peer = []
    for k in range(1, 8):
        g = lax.rem(group + k, 8)
        g_peer.append(device(g // 4, lax.rem(g, 4), z, x_hi, core))

    load_act = pltpu.make_async_copy(act_ref, act_in, loc_sem.at[0])
    load_act.start()
    load_old = pltpu.make_async_copy(old_ref, old_in, loc_sem.at[1])
    load_old.start()
    peers = z_peer + g_peer + [outer, twin]
    barrier = pltpu.get_barrier_semaphore()
    for peer in peers:
        pl.semaphore_signal(barrier, inc=1, device_id=peer, device_id_type=MESH)
    load_act.wait()
    act_t[...] = act_in[...].T
    load_old.wait()
    stats_ref[z] = old_in[...].astype(BF16)
    pl.semaphore_wait(barrier, len(peers))

    feature = swap(y)
    same = core == lax.rem(feature, 2)
    root = jnp.logical_and(same, x_hi == feature // 2)
    mid = jnp.logical_and(same, x_hi != feature // 2)
    stray = feature != mp

    def out_columns(side, chunk):
        offset, width = CHUNKS[chunk]
        return gout_ref.at[:, pl.ds(pl.multiple_of(side * 640 + offset, 128), width)]

    def g_slot(slot, chunk):
        offset, width = CHUNKS[chunk]
        return goutg.at[slot, :, pl.ds(offset, width)]

    def g_half(slot, chunk, way):
        offset, width = CHUNKS[chunk]
        return goutg.at[slot, pl.ds(way * 128, 128), pl.ds(offset, width)]

    def x_copy(chunk):
        return remote(
            out_columns(other_x, chunk), g_slot(group, chunk),
            x_send.at[chunk], x_recv.at[chunk], partner,
        )

    def x_landed(chunk):
        ref = g_slot(other_x * 4 + y, chunk)
        remote(ref, ref, x_send.at[chunk], x_recv.at[chunk], partner).wait_recv()

    def y_copy(chunk, kind, way):
        index = chunk * 8 + kind * 2 + way
        column = other_x if kind in (PAIR, ON_PAIR) else x_lo
        if kind in (OWN, PAIR):
            dst = g_slot(column * 4 + y, chunk)
            src = out_columns(x_lo, chunk) if kind == OWN else dst
        else:
            dst = g_half(column * 4 + (y_down if way == 0 else y_up), chunk, way)
            src = dst
        return remote(src, dst, g_send.at[index], g_recv.at[index], y_peer[way])

    def y_landed(chunk, kind, way):
        index = chunk * 8 + kind * 2 + way
        column = other_x if kind in (PAIR, ON_PAIR) else x_lo
        if kind in (OWN, PAIR):
            ref = g_slot(column * 4 + (y_down if way == 0 else y_up), chunk)
        else:
            ref = g_half(column * 4 + y_far, chunk, way)
        remote(ref, ref, g_send.at[index], g_recv.at[index], y_peer[way]).wait_recv()

    def y_send(chunk, kind):
        for way in range(2):
            if kind in (ON_OWN, ON_PAIR):
                y_landed(chunk, kind - 2, way)
            y_copy(chunk, kind, way).start()

    def a_slot(slot):
        return actg.at[:, pl.ds(pl.multiple_of(slot * 256, 256), 256)]

    def a_landed(slot):
        remote(a_slot(slot), a_slot(slot), a1_sem, a_recv.at[slot], partner).wait_recv()

    def a_send(slot, index, peer, src=None):
        src = a_slot(slot) if src is None else src
        return remote(src, a_slot(slot), a2_send.at[index], a_recv.at[slot], peer)

    arrivals = (y, y_down, y_up, y_far)
    a1_copy = remote(
        act_t, a_slot(group), a1_sem, a_recv.at[group], device(x_lo, swap(mp), z, x_hi, core)
    )

    def from_root(i):
        slot = x_lo * 4 + arrivals[i]
        if i > 0:
            a_landed(slot)
        src = act_t if i == 0 else None
        a_send(slot, i, partner, src).start()
        a_send(slot, 12 + i, outer, src).start()
        a_send(slot, 4 + i, twin, src).start()

    def from_mid(i):
        slot = other_x * 4 + arrivals[i]
        a_landed(slot)
        a_send(slot, i, partner).start()
        a_send(slot, 4 + i, twin).start()

    stats = Ring(lambda i: stats_ref.at[i], st_send, st_recv, (z_peer[0], z_peer[6]), z)

    pl.when(stray)(lambda: a1_copy.start())
    x_copy(0).start()
    pl.when(root)(lambda: from_root(0))
    y_send(0, OWN)
    stats.start(0)
    x_copy(1).start()
    keep = pltpu.make_async_copy(
        gout_ref.at[:, pl.ds(pl.multiple_of(x_lo * 640, 128), 640)], goutg.at[group], loc_sem.at[2]
    )
    keep.start()

    @pl.when(jnp.logical_not(stray))
    def _():
        actg[:, pl.ds(pl.multiple_of(group * 256, 256), 256)] = act_t[...]

    pl.when(root)(lambda: from_root(1))
    x_landed(0)
    y_send(0, PAIR)
    stats.arrived(0)
    stats.start(1)

    @pl.when(root)
    def _():
        from_root(2)
        from_root(3)

    pl.when(mid)(lambda: from_mid(0))
    y_send(1, OWN)
    x_landed(1)
    y_send(1, PAIR)
    y_send(0, ON_OWN)
    pl.when(mid)(lambda: from_mid(1))
    stats.arrived(1)
    stats.start(2)
    y_send(0, ON_PAIR)
    pl.when(mid)(lambda: from_mid(2))
    stats.arrived(2)
    stats.start(3)
    y_send(1, ON_OWN)
    pl.when(mid)(lambda: from_mid(3))
    y_send(1, ON_PAIR)

    first = jnp.where(root, x_lo, other_x)

    @pl.when(same)
    def _():
        for i in range(4):
            slot = (1 - first) * 4 + arrivals[i]
            a_landed(slot)
            a_send(slot, 8 + i, twin).start()

    @pl.when(jnp.logical_not(same))
    def _():
        for slot in range(8):
            a_landed(slot)

    keep.wait()

    def z_sum(chunk):
        offset, width = CHUNKS[chunk]
        for kind in (ON_OWN, ON_PAIR):
            for way in range(2):
                y_landed(chunk, kind, way)
        right = goutg[:, :, offset : offset + width].reshape(2048, width)
        product = jnp.dot(actg[...], right, preferred_element_type=F32)
        totals[chunk][...] = product
        parts[chunk][...] = product.astype(BF16).reshape(8, 80, width)
        sent = []
        for k in range(1, 8):
            to = lax.rem(z + k, 8)
            copy = remote(
                parts[chunk].at[to], rss[chunk].at[k],
                rs_send.at[chunk * 8 + k], rs_recv.at[chunk * 8 + k], z_peer[k - 1],
            )
            copy.start()
            sent.append(copy)
        return sent

    def group_spread(chunk, sums):
        rows = totals[chunk][pl.ds(pl.multiple_of(z * 80, 8), 80), :]
        for k in range(1, 8):
            sums[k - 1].wait_recv()
            rows = rows + rss[chunk][k].astype(F32)
        ggs[chunk][group] = rows.astype(BF16)
        sent = []
        for k in range(1, 8):
            own = ggs[chunk].at[group]
            copy = remote(
                own, own, gg_send.at[chunk * 8 + k], gg_recv.at[chunk * 8 + k], g_peer[k - 1]
            )
            copy.start()
            sent.append(copy)
        return sent

    block = jnp.int32(0)
    for b in range(8):
        block = jnp.where(owner_ref[b] == group, b // 4 * 4 + SWAP[b % 4], block)

    def pick(chunk, spread):
        offset, width = CHUNKS[chunk]
        for copy in spread:
            copy.wait_recv()
        grad_ref[z, :, offset : offset + width] = ggs[chunk][block]
        sems = ((z0_send, z0_recv), (z1_send, z1_recv))[chunk]
        ring = Ring(
            lambda i: grad_ref.at[i, :, pl.ds(offset, width)], *sems, (z_peer[0], z_peer[6]), z
        )
        ring.start(0)
        return ring

    sums0 = z_sum(0)
    sums1 = z_sum(1)
    stats.arrived(3)
    spread0 = group_spread(0, sums0)
    ring0 = pick(0, spread0)
    spread1 = group_spread(1, sums1)
    ring0.arrived(0)
    ring0.start(1)
    ring1 = pick(1, spread1)
    ring0.arrived(1)
    ring0.start(2)
    ring1.arrived(0)
    ring1.start(1)
    ring0.arrived(2)
    ring0.start(3)
    ring1.arrived(1)
    ring1.start(2)
    ring0.arrived(3)
    ring1.arrived(2)
    ring1.start(3)
    ring1.arrived(3)

    ring0.drain()
    ring1.drain()
    stats.drain()
    for copy in spread0 + spread1 + sums0 + sums1 + [x_copy(0), x_copy(1)]:
        copy.wait_send()
    for chunk in range(2):
        for kind in range(4):
            for way in range(2):
                y_copy(chunk, kind, way).wait_send()

    pl.when(stray)(lambda: a1_copy.wait_send())

    @pl.when(same)
    def _():
        for k in range(4):
            a_send(k, k, partner).wait_send()
            a_send(k, 4 + k, twin).wait_send()
            a_send(k, 8 + k, twin).wait_send()

    @pl.when(root)
    def _():
        for k in range(4):
            a_send(k, 12 + k, outer).wait_send()


def gather_gradient(activations, grad_out, old_rows, owner_map):
    dma = pltpu.SemaphoreType.DMA
    hbm = pl.BlockSpec(memory_space=pl.ANY)
    widths = [width for _, width in CHUNKS]
    return pl.pallas_call(
        gather_kernel,
        out_shape=(
            jax.ShapeDtypeStruct((8, 80, 640), BF16),
            jax.ShapeDtypeStruct((8, 160, 640), BF16),
        ),
        in_specs=[hbm, hbm, hbm, SMEM],
        out_specs=(VMEM, VMEM),
        scratch_shapes=[
            pltpu.VMEM((256, 640), BF16),
            pltpu.VMEM((640, 256), BF16),
            pltpu.VMEM((160, 640), F32),
            pltpu.VMEM((640, 2048), BF16),
            pltpu.VMEM((8, 256, 640), BF16),
            *[pltpu.VMEM((640, width), F32) for width in widths],
            *[pltpu.VMEM((8, 80, width), BF16) for _ in range(3) for width in widths],
            dma((2,)), dma((2,)), dma, dma((16,)), dma((8,)), dma((16,)), dma((16,)),
            dma((7,)), dma((7,)), dma((16,)), dma((16,)), dma((16,)), dma((16,)),
            dma((7,)), dma((7,)), dma((7,)), dma((7,)), dma((3,)),
        ],
        compiler_params=pltpu.CompilerParams(
            collective_id=0, has_side_effects=True, vmem_limit_bytes=32 * 2**20
        ),
        name="gather_gradient",
    )(activations, grad_out, old_rows, owner_map)


def dot(a, b):
    return jnp.dot(a, b, preferred_element_type=F32)


def finish_kernel(
    grad_ref, stats_ref, old_ref, rotation_ref, update_ref, stats_out, roots_out,
    both, moment, wide, low1, low2, low3, low_w, scales, rot0, rot1, rot2,
    a_send, a_recv, az_send, az_recv, ay_send, ay_recv, bz_send, bz_recv,
    x_send, x_recv, y_send, y_recv, p_send, p_recv, f_send, f_recv, q_send, q_recv,
    c_send, c_recv, rot_send, rot_recv,
):
    x_lo, y, z, x_hi, core = place()
    group = x_lo * 4 + y
    other_x = 1 - x_lo
    pair = other_x * 4 + y
    y_up, y_down, y_far = lax.rem(y + 1, 4), lax.rem(y + 3, 4), lax.rem(y + 2, 4)
    partner = device(other_x, y, z, x_hi, core)
    up_y = device(x_lo, y_up, z, x_hi, core)
    down_y = device(x_lo, y_down, z, x_hi, core)
    up_z = device(x_lo, y, lax.rem(z + 1, 8), x_hi, core)
    down_z = device(x_lo, y, lax.rem(z + 7, 8), x_hi, core)
    g_peer = []
    for k in range(1, 8):
        g = lax.rem(group + k, 8)
        g_peer.append(device(g // 4, lax.rem(g, 4), z, x_hi, core))
    peers = g_peer + [up_z, down_z]
    barrier = pltpu.get_barrier_semaphore()
    for peer in peers:
        pl.semaphore_signal(barrier, inc=1, device_id=peer, device_id_type=MESH)

    rots = (rot0, rot1, rot2)

    def rotate(step):
        return remote(
            rots[step].at[0], rots[step].at[1], rot_send.at[step], rot_recv.at[step],
            g_peer[(1 << step) - 1],
        )

    def rotated(step):
        rotate(step).wait_recv()
        bit = lax.rem(rotation_ref[0] // (1 << step), 2)
        return rots[step][bit]

    side = z // 4
    quarter = pl.multiple_of(lax.rem(z, 4) * 160, 16)
    eighth = pl.multiple_of(z * 80, 16)
    grad = grad_ref[...].reshape(640, 640)
    both[0] = grad
    both[1] = grad.T

    own = dot(both[side, pl.ds(quarter, 160), :], both[1 - side])
    stats_out[...] = BETA * old_ref[...] + (1.0 - BETA) * own

    def start(s, carry):
        a = BETA * stats_ref[s].astype(F32) + (1.0 - BETA) * dot(both[s], both[1 - s])
        moment[s] = a
        norm = jnp.sqrt(jnp.sum(a * a, keepdims=True))
        scale = 2.5 / norm
        scales[s] = jnp.broadcast_to(jnp.sqrt(jnp.sqrt(scale)), (8, 128))
        m = moment[s] * scale
        moment[s] = m
        low1[s] = m.astype(BF16)
        return carry

    lax.fori_loop(0, 2, start, 0)

    def advance(now, later):
        def square(s, carry):
            w = dot(now[s], now[s]) - 10.0 * moment[s]
            wide[s] = w
            low_w[s] = w.astype(BF16)
            return carry

        def fourth(s, carry):
            h = dot(low_w[s], low_w[s]) + 50.0 * wide[s]
            wide[s] = h
            return carry

        def finish(s, carry):
            m = (625.0 * moment[s] + dot(now[s], wide[s].astype(BF16))) * (1.0 / 256.0)
            moment[s] = m
            later[s] = m.astype(BF16)
            return carry

        lax.fori_loop(0, 2, square, 0)
        lax.fori_loop(0, 2, fourth, 0)
        lax.fori_loop(0, 2, finish, 0)

    advance(low1, low2)
    advance(low2, low3)

    def factor(r, low, s):
        return 1.25 * r - 0.25 * dot(r.astype(BF16), low[s])

    def chain(r, s):
        r = factor(r, low2, s)
        r = factor(r, low3, s)
        t = r
        for _ in range(4):
            t = factor(t, low3, s)
        return 1.25 * r - 0.25 * dot(t.astype(BF16), low3[s])

    def identity(rows, offset):
        across = lax.broadcasted_iota(jnp.int32, (rows, 640), 1)
        down = lax.broadcasted_iota(jnp.int32, (rows, 640), 0) + offset
        return (across == down).astype(F32)

    def first(rows, offset, s):
        m = low1[s, pl.ds(offset, rows), :].astype(F32)
        return (1.25 * identity(rows, offset) - 0.25 * m) * scales[s, 0:1, 0:1]

    rot0[0] = chain(first(160, quarter, side), side).astype(BF16)
    pl.semaphore_wait(barrier, len(peers))
    rotate(0).start()
    left = chain(first(80, eighth, 0), 0)
    rot1[0] = rotated(0)
    rotate(1).start()
    high = left.astype(BF16)
    low = (left - high.astype(F32)).astype(BF16)
    right = dot(high, both[0]) + dot(low, both[0])
    right = factor(right, low1, 1) * scales[1, 0:1, 0:1]
    right = chain(right, 1)
    rot2[0] = rotated(1)
    rotate(2).start()
    update_ref[group, z] = right.astype(BF16)

    def slot(r):
        return lax.rem(z + r, 8)

    def rows(g, r, start, count):
        return update_ref.at[g, slot(r), pl.ds(start, count)]

    sent = []

    def send(ref, sems, index, peer):
        copy = remote(ref, ref, sems[0].at[index], sems[1].at[index], peer)
        copy.start()
        sent.append(copy)

    def landed(ref, sems, index):
        remote(ref, ref, sems[0].at[index], sems[1].at[index], partner).wait_recv()

    xs, ys, ps = (x_send, x_recv), (y_send, y_recv), (p_send, p_recv)
    fs, qs, cs = (f_send, f_recv), (q_send, q_recv), (c_send, c_recv)
    low, high, far = x_lo * 4 + y_down, x_lo * 4 + y_up, x_lo * 4 + y_far
    p_low, p_high, p_far = other_x * 4 + y_down, other_x * 4 + y_up, other_x * 4 + y_far

    ring_b = Ring(
        lambda i: update_ref.at[group, i, pl.ds(32, 48)], bz_send, bz_recv, (up_z, down_z), z
    )
    ring_a = Ring(
        lambda i: update_ref.at[pl.ds(0, 4), i, pl.ds(0, 32)], az_send, az_recv, (up_z, down_z), z
    )
    ring_c = Ring(
        lambda i: update_ref.at[pl.ds(4, 4), i, pl.ds(0, 32)], ay_send, ay_recv, (up_z, down_z), z
    )

    def own_out(r):
        send(rows(group, r, 32, 48), xs, r, partner)
        send(rows(group, r, 32, 48), ys, r, up_y)
        send(rows(group, r, 32, 48), ys, 8 + r, down_y)

    def pair_out(r):
        landed(rows(pair, r, 32, 48), xs, r)
        send(rows(pair, r, 32, 32), ps, r, up_y)
        send(rows(pair, r, 32, 32), ps, 8 + r, down_y)

    def own_on(r):
        landed(rows(low, r, 32, 48), ys, r)
        if r < 4:
            send(rows(low, r, 32, 48), fs, r, up_y)
        landed(rows(high, r, 32, 48), ys, 8 + r)
        if r >= 4:
            send(rows(high, r, 32, 48), fs, r, down_y)

    def pair_on(r):
        landed(rows(p_low, r, 32, 32), ps, r)
        if r < 4:
            send(rows(p_low, r, 32, 32), qs, r, up_y)
        landed(rows(p_high, r, 32, 32), ps, 8 + r)
        if r >= 4:
            send(rows(p_high, r, 32, 32), qs, r, down_y)

    def across(g, index):
        send(update_ref.at[g, :, pl.ds(64, 16)], cs, index, partner)

    ring_b.start(0)
    over = []
    for k in range(1, 8):
        own = update_ref.at[group, z, pl.ds(0, 32)]
        copy = remote(own, own, a_send.at[k], a_recv.at[k], g_peer[k - 1])
        copy.start()
        over.append(copy)
    own_out(0)

    ring_b.arrived(0)
    ring_b.start(1)
    own_out(7)
    own_out(1)
    pair_out(0)
    ring_b.arrived(1)
    ring_b.start(2)
    own_out(6)
    own_out(2)
    for copy in over:
        copy.wait_recv()
    ring_a.start(0)
    ring_c.start(0)
    pair_out(7)
    pair_out(1)
    ring_b.arrived(2)
    ring_b.start(3)
    own_out(5)
    own_out(3)
    own_on(0)
    pair_out(6)
    pair_out(2)
    ring_b.arrived(3)
    own_out(4)
    own_on(7)
    own_on(1)
    pair_out(5)
    pair_out(3)
    ring_a.arrived(0)
    ring_a.start(1)
    ring_c.arrived(0)
    ring_c.start(1)
    own_on(6)
    own_on(2)
    pair_out(4)
    own_on(5)
    own_on(3)
    own_on(4)
    across(low, 0)
    across(high, 1)
    pair_on(0)
    pair_on(7)
    pair_on(1)
    ring_a.arrived(1)
    ring_a.start(2)
    ring_c.arrived(1)
    ring_c.start(2)
    for r in (6, 2, 5, 3, 4):
        pair_on(r)
    for r in range(8):
        landed(rows(far, r, 32, 48), fs, r)
    across(far, 2)
    ring_a.arrived(2)
    ring_a.start(3)
    ring_c.arrived(2)
    ring_c.start(3)
    roots_out[...] = rotated(2).astype(F32)
    for r in range(8):
        landed(rows(p_far, r, 32, 32), qs, r)
    for index, g in enumerate((p_low, p_high, p_far)):
        landed(update_ref.at[g, :, pl.ds(64, 16)], cs, index)
    ring_a.arrived(3)
    ring_c.arrived(3)

    ring_a.drain()
    ring_b.drain()
    ring_c.drain()
    for copy in sent + over:
        copy.wait_send()
    for step in range(3):
        rotate(step).wait_send()


def finish(grad, stats, old_rows, rotation):
    dma = pltpu.SemaphoreType.DMA
    return pl.pallas_call(
        finish_kernel,
        out_shape=(
            jax.ShapeDtypeStruct((8, 8, 80, 640), BF16),
            jax.ShapeDtypeStruct((160, 640), F32),
            jax.ShapeDtypeStruct((160, 640), F32),
        ),
        in_specs=[VMEM, VMEM, VMEM, SMEM],
        out_specs=(VMEM, VMEM, VMEM),
        scratch_shapes=[
            pltpu.VMEM((2, 640, 640), BF16),
            pltpu.VMEM((2, 640, 640), F32),
            pltpu.VMEM((2, 640, 640), F32),
            pltpu.VMEM((2, 640, 640), BF16),
            pltpu.VMEM((2, 640, 640), BF16),
            pltpu.VMEM((2, 640, 640), BF16),
            pltpu.VMEM((2, 640, 640), BF16),
            pltpu.VMEM((2, 8, 128), F32),
            pltpu.VMEM((2, 160, 640), BF16),
            pltpu.VMEM((2, 160, 640), BF16),
            pltpu.VMEM((2, 160, 640), BF16),
            dma((8,)), dma((8,)), dma((7,)), dma((7,)), dma((7,)), dma((7,)), dma((7,)), dma((7,)),
            dma((8,)), dma((8,)), dma((16,)), dma((16,)), dma((16,)), dma((16,)),
            dma((8,)), dma((8,)), dma((8,)), dma((8,)), dma((3,)), dma((3,)), dma((3,)), dma((3,)),
        ],
        compiler_params=pltpu.CompilerParams(
            collective_id=1, has_side_effects=True, vmem_limit_bytes=36 * 2**20
        ),
        name="finish",
    )(grad, stats, old_rows, rotation)


def order_kernel(owner_ref, in_ref, out_ref, sems):
    copies = []
    for b in range(8):
        copy = pltpu.make_async_copy(in_ref.at[owner_ref[b]], out_ref.at[b], sems.at[b])
        copy.start()
        copies.append(copy)
    for copy in copies:
        copy.wait()


def order_blocks(by_place, owner_map):
    return pl.pallas_call(
        order_kernel,
        out_shape=jax.ShapeDtypeStruct((8, 640, 640), BF16),
        in_specs=[SMEM, VMEM],
        out_specs=pl.BlockSpec(memory_space=pl.ANY),
        scratch_shapes=[pltpu.SemaphoreType.DMA((8,))],
        compiler_params=pltpu.CompilerParams(vmem_limit_bytes=16 * 2**20),
        name="order_blocks",
    )(owner_map, by_place)


def local(activations, grad_out, stats_old, owner_map, rotation):
    old_rows = stats_old.reshape(160, 640)
    grad, stats = gather_gradient(activations, grad_out, old_rows, owner_map)
    by_place, stats_new, roots_new = finish(
        grad, stats.reshape(2, 640, 640), old_rows, rotation
    )
    update = order_blocks(by_place.reshape(8, 640, 640), owner_map)
    return (
        update.reshape(2, 2560, 640),
        stats_new.reshape(stats_old.shape),
        roots_new.reshape(stats_old.shape),
    )


def solution(mesh):
    return jax.shard_map(
        local,
        mesh=mesh,
        in_specs=(P("dp", "mp"), P("dp", "mp"), P("mp", None, "dp", None, None), P(), P()),
        out_specs=(
            P("mp", None, None),
            P("mp", None, "dp", None, None),
            P("mp", None, "dp", None, None),
        ),
        check_vma=False,
    )
```

time: 185 us -> 170 us (0.919); the launches traced: 181 us -> 170 us
  Pallas kernels: 175 us -> 161 us
  local copies, waits for them, and re-layouts: 4.46 us -> 6.86 us
    pallas_call x1, Pallas kernels: 8.67 us -> 3.37 us  [order_blocks(): pl.pallas_call(order_kernel, out_shape=jax.ShapeDtypeStruct((8, 640, 640)...]
    pallas_call x2 -> x1, Pallas kernels: 75.7 us -> 71.4 us  [finish(): pl.pallas_call(finish_kernel, out_shape=(jax.ShapeDtypeStruct((8, 8, 80,...]
    pallas_call x1, Pallas kernels: 90.1 us -> 86.7 us  [gather_gradient(): pl.pallas_call(gather_kernel, out_shape=(jax.ShapeDtypeStruct((8, 80, 640...]
    unnamed x9 -> x14, local copies, waits for them, and re-layouts: 4.46 us -> 6.86 us
where the time goes in v2:
time: 170 us
  Pallas kernels  161 us (95%)
  local copies, waits for them, and re-layouts  6.86 us (4%)
    pallas_call x1, Pallas kernels, gather_gradient(): pl.pallas_call(gather_kernel, out_shape=(jax.ShapeDtypeStruct((8, 80, 640...  86.7 us
    pallas_call x1, Pallas kernels, finish(): pl.pallas_call(finish_kernel, out_shape=(jax.ShapeDtypeStruct((8, 8, 80,...  71.4 us
    unnamed x14, local copies, waits for them, and re-layouts  6.86 us

profile of v2, /device:TPU:4, one launch (start us, length us, event | category | flops | bytes accessed | tf_op | source)
XLA Modules:
  0.0 169.6 jit_solution(6698600046747582211)
XLA Ops:
  1.3 0.0 copy-start
  1.3 1.0 copy-done
  2.3 0.0 copy-start.2
  2.3 1.1 copy-done.2
  3.4 0.0 copy-start.3
  3.4 1.0 copy-done.3
  4.3 0.0 copy-start.4
  4.3 0.7 copy-done.4
  5.0 86.7 %gather_gradient.1 = (bf16[8,80,640]{2,1,0:T(8,128)(2,1)S(1)}, bf16[8,160,640]{2,1,0:T(8,128)(2,1)S(1)}) custom-call(bf16[256,640]{1,0:T(8,128)(2,1)S(1)} %copy-done.3, bf16[256,1280]{1,0:T(8,128)(2,1)S(1)} %copy-done.2, f32[160,640]{1,0:T(8,128)S(1)} %bitcast.7, s32[8]{0:T(128)S(1)} %copy-done.4), custom_call_target="tpu_custom_call" | custom-call | tf_op jit(solution)/shard_map/gather_gradient/pallas_call | solution.py:358
  91.7 0.0 copy-start.1
  91.7 1.0 copy-done.1
  92.7 71.4 %finish.1 = (bf16[8,8,80,640]{3,2,1,0:T(8,128)(2,1)S(1)}, f32[160,640]{1,0:T(8,128)S(1)}, f32[160,640]{1,0:T(8,128)S(1)}) custom-call(bf16[8,80,640]{2,1,0:T(8,128)(2,1)S(1)} %get-tuple-element.8.grad_ref, bf16[2,640,640]{2,1,0:T(8,128)(2,1)S(1)} %bitcast.9, f32[160,640]{1,0:T(8,128)S(1)} %bitcast.8, s32[1]{0:T(128)S(6)} %copy.10.rotation_ref), custom_call_target="tpu_custom_call" | custom-call | tf_op jit(solution)/shard_map/finish/pallas_call | solution.py:655
  164.1 0.0 copy-start.5
  164.1 0.6 copy-done.5
  164.7 3.4 %order_blocks.1 = bf16[8,640,640]{2,1,0:T(8,128)(2,1)} custom-call(s32[8]{0:T(128)S(1)} %copy-done.5, bf16[8,640,640]{2,1,0:T(8,128)(2,1)S(1)} %bitcast.6), custom_call_target="tpu_custom_call" | custom-call | tf_op jit(solution)/shard_map/order_blocks/pallas_call | solution.py:698
  168.1 0.8 copy.11
  168.8 0.8 copy.12
Async XLA Ops:
  1.3 1.0 copy-start
  2.3 1.1 copy-start.2
  3.4 1.0 copy-start.3
  4.3 0.7 copy-start.4
  91.7 1.0 copy-start.1
  164.1 0.7 copy-start.5

commit v3 on v2

--- a/solution.py
+++ b/solution.py
@@ -62,6 +62,46 @@
                 self.copy_down(step).wait_send()
 
 
+class Near:
+    def __init__(self, piece, send, recv, peers, z):
+        self.piece, self.send, self.recv, self.peers = piece, send, recv, peers
+        self.z = z
+
+    def copy(self, index):
+        ahead, behind, part = (
+            (2, 0, 0), (-2, 0, 0), (1, 0, 0), (-1, 0, 0), (1, 2, 0), (-1, 2, 0), (2, 2, 1), (-2, 2, 2)
+        )[index]
+        way = 1 if ahead > 0 else -1
+        ref = self.piece(lax.rem(self.z - way * behind + 8, 8), part)
+        return remote(ref, ref, self.send.at[index], self.recv.at[index], self.peers[ahead % 8 - 1])
+
+    def landed(self, index):
+        ahead, behind, part = (
+            (2, 0, 0), (-2, 0, 0), (1, 0, 0), (-1, 0, 0), (1, 2, 0), (-1, 2, 0), (2, 2, 1), (-2, 2, 2)
+        )[index]
+        way = 1 if ahead > 0 else -1
+        ref = self.piece(lax.rem(self.z - ahead - way * behind + 8, 8), part)
+        remote(ref, ref, self.send.at[index], self.recv.at[index], self.peers[0]).wait_recv()
+
+    def start(self):
+        for index in range(4):
+            self.copy(index).start()
+
+    def relay(self):
+        for index in (0, 1):
+            self.landed(index)
+            self.copy(4 + index).start()
+            self.copy(6 + index).start()
+
+    def finish(self):
+        for index in (2, 3, 4, 5, 6, 7):
+            self.landed(index)
+
+    def drain(self):
+        for index in range(8):
+            self.copy(index).wait_send()
+
+
 def swap(v):
     return lax.rem(v, 2) * 2 + v // 2
 
@@ -71,9 +111,9 @@
 OWN, PAIR, ON_OWN, ON_PAIR = range(4)
 
 
-def gather_kernel(
-    act_ref, gout_ref, old_ref, owner_ref, grad_ref, stats_ref,
-    act_in, act_t, old_in, actg, goutg, total0, total1, part0, part1, rs0, rs1, gg0, gg1,
+def gather_part(
+    act_ref, gout_ref, old_ref, owner_ref, grad_ref, stats_ref, old_in,
+    act_in, act_t, actg, goutg, total0, total1, part0, part1, rs0, rs1, gg0, gg1,
     x_send, x_recv, a1_sem, a2_send, a_recv, g_send, g_recv,
     st_send, st_recv, rs_send, rs_recv, gg_send, gg_recv, z0_send, z0_recv, z1_send, z1_recv,
     loc_sem,
@@ -298,95 +338,60 @@
             copy.wait_recv()
         grad_ref[z, :, offset : offset + width] = ggs[chunk][block]
         sems = ((z0_send, z0_recv), (z1_send, z1_recv))[chunk]
-        ring = Ring(
-            lambda i: grad_ref.at[i, :, pl.ds(offset, width)], *sems, (z_peer[0], z_peer[6]), z
-        )
-        ring.start(0)
-        return ring
+
+        def piece(i, part):
+            start, count = ((0, 80), (0, 48), (48, 32))[part]
+            return grad_ref.at[i, pl.ds(start, count), pl.ds(offset, width)]
+
+        near = Near(piece, *sems, z_peer, z)
+        near.start()
+        return near
 
     sums0 = z_sum(0)
     sums1 = z_sum(1)
     stats.arrived(3)
     spread0 = group_spread(0, sums0)
-    ring0 = pick(0, spread0)
+    near0 = pick(0, spread0)
     spread1 = group_spread(1, sums1)
-    ring0.arrived(0)
-    ring0.start(1)
-    ring1 = pick(1, spread1)
-    ring0.arrived(1)
-    ring0.start(2)
-    ring1.arrived(0)
-    ring1.start(1)
-    ring0.arrived(2)
-    ring0.start(3)
-    ring1.arrived(1)
-    ring1.start(2)
-    ring0.arrived(3)
-    ring1.arrived(2)
-    ring1.start(3)
-    ring1.arrived(3)
-
-    ring0.drain()
-    ring1.drain()
-    stats.drain()
-    for copy in spread0 + spread1 + sums0 + sums1 + [x_copy(0), x_copy(1)]:
-        copy.wait_send()
-    for chunk in range(2):
-        for kind in range(4):
-            for way in range(2):
-                y_copy(chunk, kind, way).wait_send()
-
-    pl.when(stray)(lambda: a1_copy.wait_send())
-
-    @pl.when(same)
-    def _():
-        for k in range(4):
-            a_send(k, k, partner).wait_send()
-            a_send(k, 4 + k, twin).wait_send()
-            a_send(k, 8 + k, twin).wait_send()
-
-    @pl.when(root)
-    def _():
-        for k in range(4):
-            a_send(k, 12 + k, outer).wait_send()
-
-
-def gather_gradient(activations, grad_out, old_rows, owner_map):
-    dma = pltpu.SemaphoreType.DMA
-    hbm = pl.BlockSpec(memory_space=pl.ANY)
-    widths = [width for _, width in CHUNKS]
-    return pl.pallas_call(
-        gather_kernel,
-        out_shape=(
-            jax.ShapeDtypeStruct((8, 80, 640), BF16),
-            jax.ShapeDtypeStruct((8, 160, 640), BF16),
-        ),
-        in_specs=[hbm, hbm, hbm, SMEM],
-        out_specs=(VMEM, VMEM),
-        scratch_shapes=[
-            pltpu.VMEM((256, 640), BF16),
-            pltpu.VMEM((640, 256), BF16),
-            pltpu.VMEM((160, 640), F32),
-            pltpu.VMEM((640, 2048), BF16),
-            pltpu.VMEM((8, 256, 640), BF16),
-            *[pltpu.VMEM((640, width), F32) for width in widths],
-            *[pltpu.VMEM((8, 80, width), BF16) for _ in range(3) for width in widths],
-            dma((2,)), dma((2,)), dma, dma((16,)), dma((8,)), dma((16,)), dma((16,)),
-            dma((7,)), dma((7,)), dma((16,)), dma((16,)), dma((16,)), dma((16,)),
-            dma((7,)), dma((7,)), dma((7,)), dma((7,)), dma((3,)),
-        ],
-        compiler_params=pltpu.CompilerParams(
-            collective_id=0, has_side_effects=True, vmem_limit_bytes=32 * 2**20
-        ),
-        name="gather_gradient",
-    )(activations, grad_out, old_rows, owner_map)
+    near0.relay()
+    near1 = pick(1, spread1)
+    near1.relay()
+    near0.finish()
+    near1.finish()
+
+    def drain():
+        near0.drain()
+        near1.drain()
+        stats.drain()
+        for copy in spread0 + spread1 + sums0 + sums1 + [x_copy(0), x_copy(1)]:
+            copy.wait_send()
+        for chunk in range(2):
+            for kind in range(4):
+                for way in range(2):
+                    y_copy(chunk, kind, way).wait_send()
+
+        pl.when(stray)(lambda: a1_copy.wait_send())
+
+        @pl.when(same)
+        def _():
+            for k in range(4):
+                a_send(k, k, partner).wait_send()
+                a_send(k, 4 + k, twin).wait_send()
+                a_send(k, 8 + k, twin).wait_send()
+
+        @pl.when(root)
+        def _():
+            for k in range(4):
+                a_send(k, 12 + k, outer).wait_send()
+
+    return drain
 
 
 def dot(a, b):
     return jnp.dot(a, b, preferred_element_type=F32)
 
 
-def finish_kernel(
+def finish_part(
     grad_ref, stats_ref, old_ref, rotation_ref, update_ref, stats_out, roots_out,
     both, moment, wide, low1, low2, low3, low_w, scales, rot0, rot1, rot2,
     a_send, a_recv, az_send, az_recv, ay_send, ay_recv, bz_send, bz_recv,
@@ -407,11 +412,7 @@
     for k in range(1, 8):
         g = lax.rem(group + k, 8)
         g_peer.append(device(g // 4, lax.rem(g, 4), z, x_hi, core))
-    peers = g_peer + [up_z, down_z]
-    barrier = pltpu.get_barrier_semaphore()
-    for peer in peers:
-        pl.semaphore_signal(barrier, inc=1, device_id=peer, device_id_type=MESH)
-
+    z_peer = [device(x_lo, y, lax.rem(z + k, 8), x_hi, core) for k in range(1, 8)]
     rots = (rot0, rot1, rot2)
 
     def rotate(step):
@@ -436,7 +437,7 @@
     stats_out[...] = BETA * old_ref[...] + (1.0 - BETA) * own
 
     def start(s, carry):
-        a = BETA * stats_ref[s].astype(F32) + (1.0 - BETA) * dot(both[s], both[1 - s])
+        a = BETA * stats_ref[pl.ds(s * 4, 4)].reshape(640, 640).astype(F32) + (1.0 - BETA) * dot(both[s], both[1 - s])
         moment[s] = a
         norm = jnp.sqrt(jnp.sum(a * a, keepdims=True))
         scale = 2.5 / norm
@@ -494,18 +495,13 @@
         return (1.25 * identity(rows, offset) - 0.25 * m) * scales[s, 0:1, 0:1]
 
     rot0[0] = chain(first(160, quarter, side), side).astype(BF16)
-    pl.semaphore_wait(barrier, len(peers))
     rotate(0).start()
     left = chain(first(80, eighth, 0), 0)
-    rot1[0] = rotated(0)
-    rotate(1).start()
     high = left.astype(BF16)
     low = (left - high.astype(F32)).astype(BF16)
     right = dot(high, both[0]) + dot(low, both[0])
     right = factor(right, low1, 1) * scales[1, 0:1, 0:1]
     right = chain(right, 1)
-    rot2[0] = rotated(1)
-    rotate(2).start()
     update_ref[group, z] = right.astype(BF16)
 
     def slot(r):
@@ -529,9 +525,11 @@
     low, high, far = x_lo * 4 + y_down, x_lo * 4 + y_up, x_lo * 4 + y_far
     p_low, p_high, p_far = other_x * 4 + y_down, other_x * 4 + y_up, other_x * 4 + y_far
 
-    ring_b = Ring(
-        lambda i: update_ref.at[group, i, pl.ds(32, 48)], bz_send, bz_recv, (up_z, down_z), z
-    )
+    def piece(i, part):
+        start, count = ((32, 48), (32, 32), (64, 16))[part]
+        return update_ref.at[group, i, pl.ds(start, count)]
+
+    near = Near(piece, bz_send, bz_recv, z_peer, z)
     ring_a = Ring(
         lambda i: update_ref.at[pl.ds(0, 4), i, pl.ds(0, 32)], az_send, az_recv, (up_z, down_z), z
     )
@@ -568,63 +566,60 @@
     def across(g, index):
         send(update_ref.at[g, :, pl.ds(64, 16)], cs, index, partner)
 
-    ring_b.start(0)
+    near.start()
+    own_out(0)
     over = []
     for k in range(1, 8):
         own = update_ref.at[group, z, pl.ds(0, 32)]
         copy = remote(own, own, a_send.at[k], a_recv.at[k], g_peer[k - 1])
         copy.start()
         over.append(copy)
-    own_out(0)
-
-    ring_b.arrived(0)
-    ring_b.start(1)
-    own_out(7)
-    own_out(1)
-    pair_out(0)
-    ring_b.arrived(1)
-    ring_b.start(2)
+
+    near.relay()
     own_out(6)
     own_out(2)
+    near.landed(2)
+    own_out(7)
+    near.landed(3)
+    own_out(1)
     for copy in over:
         copy.wait_recv()
     ring_a.start(0)
     ring_c.start(0)
-    pair_out(7)
-    pair_out(1)
-    ring_b.arrived(2)
-    ring_b.start(3)
+    rot1[0] = rotated(0)
+    rotate(1).start()
+    pair_out(0)
+    own_on(0)
+    for r in (6, 2, 7, 1):
+        pair_out(r)
+    near.landed(4)
     own_out(5)
+    near.landed(5)
     own_out(3)
-    own_on(0)
-    pair_out(6)
-    pair_out(2)
-    ring_b.arrived(3)
+    near.landed(6)
+    near.landed(7)
     own_out(4)
-    own_on(7)
-    own_on(1)
-    pair_out(5)
-    pair_out(3)
+    for r in (6, 2, 7, 1):
+        own_on(r)
     ring_a.arrived(0)
     ring_a.start(1)
     ring_c.arrived(0)
     ring_c.start(1)
-    own_on(6)
-    own_on(2)
-    pair_out(4)
-    own_on(5)
-    own_on(3)
-    own_on(4)
+    for r in (5, 3, 4):
+        pair_out(r)
+    for r in (5, 3, 4):
+        own_on(r)
     across(low, 0)
     across(high, 1)
-    pair_on(0)
-    pair_on(7)
-    pair_on(1)
+    rot2[0] = rotated(1)
+    rotate(2).start()
+    for r in (0, 6, 2, 7, 1):
+        pair_on(r)
     ring_a.arrived(1)
     ring_a.start(2)
     ring_c.arrived(1)
     ring_c.start(2)
-    for r in (6, 2, 5, 3, 4):
+    for r in (5, 3, 4):
         pair_on(r)
     for r in range(8):
         landed(rows(far, r, 32, 48), fs, r)
@@ -641,8 +636,8 @@
     ring_a.arrived(3)
     ring_c.arrived(3)
 
+    near.drain()
     ring_a.drain()
-    ring_b.drain()
     ring_c.drain()
     for copy in sent + over:
         copy.wait_send()
@@ -650,18 +645,51 @@
         rotate(step).wait_send()
 
 
-def finish(grad, stats, old_rows, rotation):
-    dma = pltpu.SemaphoreType.DMA
+GATHER_REFS = 30
+
+
+def step_kernel(
+    act_ref, gout_ref, old_ref, owner_ref, rotation_ref, update_ref, stats_out, roots_out,
+    grad_ref, stats_ref, old_in, *rest,
+):
+    drain = gather_part(
+        act_ref, gout_ref, old_ref, owner_ref, grad_ref, stats_ref, old_in, *rest[:GATHER_REFS]
+    )
+    finish_part(
+        grad_ref, stats_ref, old_in, rotation_ref, update_ref, stats_out, roots_out,
+        *rest[GATHER_REFS:],
+    )
+    drain()
+
+
+def shampoo_step(activations, grad_out, old_rows, owner_map, rotation):
+    hbm = pl.BlockSpec(memory_space=pltpu.HBM)
+    widths = [width for _, width in CHUNKS]
+
+    def sems(*counts):
+        return [pltpu.SemaphoreType.DMA((count,)) for count in counts]
+
     return pl.pallas_call(
-        finish_kernel,
+        step_kernel,
         out_shape=(
             jax.ShapeDtypeStruct((8, 8, 80, 640), BF16),
             jax.ShapeDtypeStruct((160, 640), F32),
             jax.ShapeDtypeStruct((160, 640), F32),
         ),
-        in_specs=[VMEM, VMEM, VMEM, SMEM],
+        in_specs=[hbm, hbm, hbm, SMEM, SMEM],
         out_specs=(VMEM, VMEM, VMEM),
         scratch_shapes=[
+            pltpu.VMEM((8, 80, 640), BF16),
+            pltpu.VMEM((8, 160, 640), BF16),
+            pltpu.VMEM((160, 640), F32),
+            pltpu.VMEM((256, 640), BF16),
+            pltpu.VMEM((640, 256), BF16),
+            pltpu.VMEM((640, 2048), BF16),
+            pltpu.VMEM((8, 256, 640), BF16),
+            *[pltpu.VMEM((640, width), F32) for width in widths],
+            *[pltpu.VMEM((8, 80, width), BF16) for _ in range(3) for width in widths],
+            *sems(2, 2), pltpu.SemaphoreType.DMA,
+            *sems(16, 8, 16, 16, 7, 7, 16, 16, 16, 16, 8, 8, 8, 8, 3),
             pltpu.VMEM((2, 640, 640), BF16),
             pltpu.VMEM((2, 640, 640), F32),
             pltpu.VMEM((2, 640, 640), F32),
@@ -673,46 +701,52 @@
             pltpu.VMEM((2, 160, 640), BF16),
             pltpu.VMEM((2, 160, 640), BF16),
             pltpu.VMEM((2, 160, 640), BF16),
-            dma((8,)), dma((8,)), dma((7,)), dma((7,)), dma((7,)), dma((7,)), dma((7,)), dma((7,)),
-            dma((8,)), dma((8,)), dma((16,)), dma((16,)), dma((16,)), dma((16,)),
-            dma((8,)), dma((8,)), dma((8,)), dma((8,)), dma((3,)), dma((3,)), dma((3,)), dma((3,)),
+            *sems(8, 8, 7, 7, 7, 7, 8, 8, 8, 8, 16, 16, 16, 16, 8, 8, 8, 8, 3, 3, 3, 3),
         ],
         compiler_params=pltpu.CompilerParams(
-            collective_id=1, has_side_effects=True, vmem_limit_bytes=36 * 2**20
+            collective_id=0, has_side_effects=True, vmem_limit_bytes=44 * 2**20
         ),
-        name="finish",
-    )(grad, stats, old_rows, rotation)
-
-
-def order_kernel(owner_ref, in_ref, out_ref, sems):
-    copies = []
-    for b in range(8):
-        copy = pltpu.make_async_copy(in_ref.at[owner_ref[b]], out_ref.at[b], sems.at[b])
+        name="shampoo_step",
+    )(activations, grad_out, old_rows, owner_map, rotation)
+
+
+def order_kernel(owner_ref, in_ref, stats_ref, roots_ref, out_ref, stats_out, roots_out, sems):
+    copies = [
+        pltpu.make_async_copy(in_ref.at[owner_ref[b]], out_ref.at[b], sems.at[b]) for b in range(8)
+    ]
+    copies.append(pltpu.make_async_copy(stats_ref, stats_out, sems.at[8]))
+    copies.append(pltpu.make_async_copy(roots_ref, roots_out, sems.at[9]))
+    for copy in copies:
         copy.start()
-        copies.append(copy)
     for copy in copies:
         copy.wait()
 
 
-def order_blocks(by_place, owner_map):
+def order_blocks(by_place, stats_new, roots_new, owner_map):
+    hbm = pl.BlockSpec(memory_space=pltpu.HBM)
     return pl.pallas_call(
         order_kernel,
-        out_shape=jax.ShapeDtypeStruct((8, 640, 640), BF16),
-        in_specs=[SMEM, VMEM],
-        out_specs=pl.BlockSpec(memory_space=pl.ANY),
-        scratch_shapes=[pltpu.SemaphoreType.DMA((8,))],
+        out_shape=(
+            jax.ShapeDtypeStruct((8, 640, 640), BF16),
+            jax.ShapeDtypeStruct((160, 640), F32),
+            jax.ShapeDtypeStruct((160, 640), F32),
+        ),
+        in_specs=[SMEM, VMEM, VMEM, VMEM],
+        out_specs=(hbm, hbm, hbm),
+        scratch_shapes=[pltpu.SemaphoreType.DMA((10,))],
         compiler_params=pltpu.CompilerParams(vmem_limit_bytes=16 * 2**20),
         name="order_blocks",
-    )(owner_map, by_place)
+    )(owner_map, by_place, stats_new, roots_new)
 
 
 def local(activations, grad_out, stats_old, owner_map, rotation):
     old_rows = stats_old.reshape(160, 640)
-    grad, stats = gather_gradient(activations, grad_out, old_rows, owner_map)
-    by_place, stats_new, roots_new = finish(
-        grad, stats.reshape(2, 640, 640), old_rows, rotation
-    )
-    update = order_blocks(by_place.reshape(8, 640, 640), owner_map)
+    by_place, stats_new, roots_new = shampoo_step(
+        activations, grad_out, old_rows, owner_map, rotation
+    )
+    update, stats_new, roots_new = order_blocks(
+        by_place.reshape(8, 640, 640), stats_new, roots_new, owner_map
+    )
     return (
         update.reshape(2, 2560, 640),
         stats_new.reshape(stats_old.shape),

time: 170 us -> 157 us (0.924)
  Pallas kernels: 161 us -> 152 us
  local copies, waits for them, and re-layouts: 6.86 us -> 3.71 us
    pallas_call x3 -> x2, Pallas kernels: 161 us -> 152 us  [the longest x1 148 us: shampoo_step(): pl.pallas_call(step_kernel, out_shape=(jax.ShapeDtypeStruct((8, 8, 80, 64...]
    unnamed x14 -> x8, local copies, waits for them, and re-layouts: 6.86 us -> 3.71 us
where the time goes in v3:
time: 157 us
  Pallas kernels  152 us (97%)
  local copies, waits for them, and re-layouts  3.71 us (2%)
    pallas_call x1, Pallas kernels, shampoo_step(): pl.pallas_call(step_kernel, out_shape=(jax.ShapeDtypeStruct((8, 8, 80, 64...  148 us
    unnamed x8, local copies, waits for them, and re-layouts  3.71 us
    pallas_call x1, Pallas kernels, order_blocks(): pl.pallas_call(order_kernel, out_shape=(jax.ShapeDtypeStruct((8, 640, 640...  3.62 us

profile of v3, /device:TPU:4, one launch (start us, length us, event | category | flops | bytes accessed | tf_op | source)
XLA Modules:
  0.0 156.7 jit_solution(14341159927602845487)
XLA Ops:
  1.3 0.0 copy-start
  1.3 1.1 copy-done
  2.4 0.0 copy-start.1
  2.4 1.0 copy-done.1
  3.4 0.0 copy-start.2
  3.4 1.0 copy-done.2
  4.3 0.0 copy-start.3
  4.3 0.7 copy-done.3
  5.0 148.0 %shampoo_step.1 = (bf16[8,8,80,640]{3,2,1,0:T(8,128)(2,1)S(1)}, f32[160,640]{1,0:T(8,128)S(1)}, f32[160,640]{1,0:T(8,128)S(1)}) custom-call(bf16[256,640]{1,0:T(8,128)(2,1)S(1)} %copy-done.2, bf16[256,1280]{1,0:T(8,128)(2,1)S(1)} %copy-done, f32[160,640]{1,0:T(8,128)S(1)} %bitcast.6, s32[8]{0:T(128)S(1)} %copy-done.3, s32[1]{0:T(128)S(6)} %copy.8.rotation_ref), custom_call_target="tpu_custom_call" | custom-call | tf_op jit(solution)/shard_map/shampoo_step/pallas_call | solution.py:672
  153.0 3.6 %order_blocks.1 = (bf16[8,640,640]{2,1,0:T(8,128)(2,1)}, f32[160,640]{1,0:T(8,128)}, f32[160,640]{1,0:T(8,128)}) custom-call(s32[8]{0:T(128)S(1)} %copy-done.3, bf16[8,640,640]{2,1,0:T(8,128)(2,1)S(1)} %bitcast.5, f32[160,640]{1,0:T(8,128)S(1)} %get-tuple-element.10.stats_ref, f32[160,640]{1,0:T(8,128)S(1)} %get-tuple-element.11.roots_ref), custom_call_target="tpu_custom_call" | custom-call | tf_op jit(solution)/shard_map/order_blocks/pallas_call | solution.py:727
Async XLA Ops:
  1.3 1.1 copy-start
  2.4 1.0 copy-start.1
  3.4 1.0 copy-start.2
  4.3 0.7 copy-start.3

commit v4 on v3

--- a/solution.py
+++ b/solution.py
@@ -30,10 +30,11 @@
 
 
 class Ring:
-    def __init__(self, slot, send, recv, peers, z):
+    def __init__(self, slot, send, recv, peers, z, down_last=False):
         self.slot, self.send, self.recv = slot, send, recv
         self.up, self.down = peers
         self.z = z
+        self.steps = (3, 4) if down_last else (4, 3)
 
     def copy_up(self, step):
         i = lax.rem(self.z - step + 8, 8)
@@ -41,25 +42,27 @@
 
     def copy_down(self, step):
         i = lax.rem(self.z + step, 8)
+        index = self.steps[0] + step
         return remote(
-            self.slot(i), self.slot(i), self.send.at[4 + step], self.recv.at[4 + step], self.down
+            self.slot(i), self.slot(i), self.send.at[index], self.recv.at[index], self.down
         )
 
+    def copies(self, step):
+        ways = ((self.copy_up, self.steps[0]), (self.copy_down, self.steps[1]))
+        return [copy(step) for copy, steps in ways if step < steps]
+
     def start(self, step):
-        self.copy_up(step).start()
-        if step < 3:
-            self.copy_down(step).start()
+        for copy in self.copies(step):
+            copy.start()
 
     def arrived(self, step):
-        self.copy_up(step).wait_recv()
-        if step < 3:
-            self.copy_down(step).wait_recv()
+        for copy in self.copies(step):
+            copy.wait_recv()
 
     def drain(self):
         for step in range(4):
-            self.copy_up(step).wait_send()
-            if step < 3:
-                self.copy_down(step).wait_send()
+            for copy in self.copies(step):
+                copy.wait_send()
 
 
 class Near:
@@ -202,39 +205,48 @@
                 y_landed(chunk, kind - 2, way)
             y_copy(chunk, kind, way).start()
 
-    def a_slot(slot):
-        return actg.at[:, pl.ds(pl.multiple_of(slot * 256, 256), 256)]
-
-    def a_landed(slot):
-        remote(a_slot(slot), a_slot(slot), a1_sem, a_recv.at[slot], partner).wait_recv()
-
-    def a_send(slot, index, peer, src=None):
-        src = a_slot(slot) if src is None else src
-        return remote(src, a_slot(slot), a2_send.at[index], a_recv.at[slot], peer)
+    def a_slot(slot, part):
+        return actg.at[pl.ds(part * 320, 320), pl.ds(pl.multiple_of(slot * 256, 256), 256)]
+
+    def a_copy(slot, part, send, peer, own=False):
+        dst = a_slot(slot, part)
+        src = act_t.at[pl.ds(part * 320, 320)] if own else dst
+        return remote(src, dst, send, a_recv.at[slot * 2 + part], peer)
+
+    def a_landed(slot, part):
+        a_copy(slot, part, a1_sem.at[part], partner).wait_recv()
+
+    def a_send(slot, part, index, peer, own=False):
+        return a_copy(slot, part, a2_send.at[index * 2 + part], peer, own)
 
     arrivals = (y, y_down, y_up, y_far)
-    a1_copy = remote(
-        act_t, a_slot(group), a1_sem, a_recv.at[group], device(x_lo, swap(mp), z, x_hi, core)
-    )
+    def a1_copy(part):
+        target = device(x_lo, swap(mp), z, x_hi, core)
+        return a_copy(group, part, a1_sem.at[part], target, True)
 
     def from_root(i):
         slot = x_lo * 4 + arrivals[i]
-        if i > 0:
-            a_landed(slot)
-        src = act_t if i == 0 else None
-        a_send(slot, i, partner, src).start()
-        a_send(slot, 12 + i, outer, src).start()
-        a_send(slot, 4 + i, twin, src).start()
+        for part in range(2):
+            if i > 0:
+                a_landed(slot, part)
+            a_send(slot, part, i, partner, i == 0).start()
+            a_send(slot, part, 12 + i, outer, i == 0).start()
+            a_send(slot, part, 4 + i, twin, i == 0).start()
 
     def from_mid(i):
         slot = other_x * 4 + arrivals[i]
-        a_landed(slot)
-        a_send(slot, i, partner).start()
-        a_send(slot, 4 + i, twin).start()
+        for part in range(2):
+            a_landed(slot, part)
+            a_send(slot, part, i, partner).start()
+            a_send(slot, part, 4 + i, twin).start()
 
     stats = Ring(lambda i: stats_ref.at[i], st_send, st_recv, (z_peer[0], z_peer[6]), z)
 
-    pl.when(stray)(lambda: a1_copy.start())
+    @pl.when(stray)
+    def _():
+        a1_copy(0).start()
+        a1_copy(1).start()
+
     x_copy(0).start()
     pl.when(root)(lambda: from_root(0))
     y_send(0, OWN)
@@ -282,13 +294,15 @@
     def _():
         for i in range(4):
             slot = (1 - first) * 4 + arrivals[i]
-            a_landed(slot)
-            a_send(slot, 8 + i, twin).start()
+            for part in range(2):
+                a_landed(slot, part)
+                a_send(slot, part, 8 + i, twin).start()
 
     @pl.when(jnp.logical_not(same))
     def _():
         for slot in range(8):
-            a_landed(slot)
+            a_landed(slot, 0)
+            a_landed(slot, 1)
 
     keep.wait()
 
@@ -370,19 +384,24 @@
                 for way in range(2):
                     y_copy(chunk, kind, way).wait_send()
 
-        pl.when(stray)(lambda: a1_copy.wait_send())
+        @pl.when(stray)
+        def _():
+            a1_copy(0).wait_send()
+            a1_copy(1).wait_send()
 
         @pl.when(same)
         def _():
             for k in range(4):
-                a_send(k, k, partner).wait_send()
-                a_send(k, 4 + k, twin).wait_send()
-                a_send(k, 8 + k, twin).wait_send()
+                for part in range(2):
+                    a_send(k, part, k, partner).wait_send()
+                    a_send(k, part, 4 + k, twin).wait_send()
+                    a_send(k, part, 8 + k, twin).wait_send()
 
         @pl.when(root)
         def _():
             for k in range(4):
-                a_send(k, 12 + k, outer).wait_send()
+                for part in range(2):
+                    a_send(k, part, 12 + k, outer).wait_send()
 
     return drain
 
@@ -433,46 +452,27 @@
     both[0] = grad
     both[1] = grad.T
 
-    own = dot(both[side, pl.ds(quarter, 160), :], both[1 - side])
-    stats_out[...] = BETA * old_ref[...] + (1.0 - BETA) * own
-
-    def start(s, carry):
-        a = BETA * stats_ref[pl.ds(s * 4, 4)].reshape(640, 640).astype(F32) + (1.0 - BETA) * dot(both[s], both[1 - s])
+    def advance(now, later, s):
+        w = dot(now[s], now[s]) - 10.0 * moment[s]
+        wide[s] = w
+        low_w[s] = w.astype(BF16)
+        h = dot(low_w[s], low_w[s]) + 50.0 * wide[s]
+        low_w[s] = h.astype(BF16)
+        m = (625.0 * moment[s] + dot(now[s], low_w[s])) * (1.0 / 256.0)
+        moment[s] = m
+        later[s] = m.astype(BF16)
+
+    def grow(s):
+        old = stats_ref[pl.ds(s * 4, 4)].reshape(640, 640).astype(F32)
+        a = BETA * old + (1.0 - BETA) * dot(both[s], both[1 - s])
         moment[s] = a
-        norm = jnp.sqrt(jnp.sum(a * a, keepdims=True))
-        scale = 2.5 / norm
+        scale = 2.5 / jnp.sqrt(jnp.sum(a * a, keepdims=True))
         scales[s] = jnp.broadcast_to(jnp.sqrt(jnp.sqrt(scale)), (8, 128))
         m = moment[s] * scale
         moment[s] = m
         low1[s] = m.astype(BF16)
-        return carry
-
-    lax.fori_loop(0, 2, start, 0)
-
-    def advance(now, later):
-        def square(s, carry):
-            w = dot(now[s], now[s]) - 10.0 * moment[s]
-            wide[s] = w
-            low_w[s] = w.astype(BF16)
-            return carry
-
-        def fourth(s, carry):
-            h = dot(low_w[s], low_w[s]) + 50.0 * wide[s]
-            wide[s] = h
-            return carry
-
-        def finish(s, carry):
-            m = (625.0 * moment[s] + dot(now[s], wide[s].astype(BF16))) * (1.0 / 256.0)
-            moment[s] = m
-            later[s] = m.astype(BF16)
-            return carry
-
-        lax.fori_loop(0, 2, square, 0)
-        lax.fori_loop(0, 2, fourth, 0)
-        lax.fori_loop(0, 2, finish, 0)
-
-    advance(low1, low2)
-    advance(low2, low3)
+        advance(low1, low2, s)
+        advance(low2, low3, s)
 
     def factor(r, low, s):
         return 1.25 * r - 0.25 * dot(r.astype(BF16), low[s])
@@ -494,9 +494,13 @@
         m = low1[s, pl.ds(offset, rows), :].astype(F32)
         return (1.25 * identity(rows, offset) - 0.25 * m) * scales[s, 0:1, 0:1]
 
+    grow(side)
     rot0[0] = chain(first(160, quarter, side), side).astype(BF16)
     rotate(0).start()
+    grow(1 - side)
     left = chain(first(80, eighth, 0), 0)
+    rot1[0] = rotated(0)
+    rotate(1).start()
     high = left.astype(BF16)
     low = (left - high.astype(F32)).astype(BF16)
     right = dot(high, both[0]) + dot(low, both[0])
@@ -534,7 +538,7 @@
         lambda i: update_ref.at[pl.ds(0, 4), i, pl.ds(0, 32)], az_send, az_recv, (up_z, down_z), z
     )
     ring_c = Ring(
-        lambda i: update_ref.at[pl.ds(4, 4), i, pl.ds(0, 32)], ay_send, ay_recv, (up_z, down_z), z
+        lambda i: update_ref.at[pl.ds(4, 4), i, pl.ds(0, 32)], ay_send, ay_recv, (up_z, down_z), z, True
     )
 
     def own_out(r):
@@ -575,6 +579,8 @@
         copy.start()
         over.append(copy)
 
+    own = dot(both[side, pl.ds(quarter, 160), :], both[1 - side])
+    stats_out[...] = BETA * old_ref[...] + (1.0 - BETA) * own
     near.relay()
     own_out(6)
     own_out(2)
@@ -586,8 +592,6 @@
         copy.wait_recv()
     ring_a.start(0)
     ring_c.start(0)
-    rot1[0] = rotated(0)
-    rotate(1).start()
     pair_out(0)
     own_on(0)
     for r in (6, 2, 7, 1):
@@ -688,8 +692,7 @@
             pltpu.VMEM((8, 256, 640), BF16),
             *[pltpu.VMEM((640, width), F32) for width in widths],
             *[pltpu.VMEM((8, 80, width), BF16) for _ in range(3) for width in widths],
-            *sems(2, 2), pltpu.SemaphoreType.DMA,
-            *sems(16, 8, 16, 16, 7, 7, 16, 16, 16, 16, 8, 8, 8, 8, 3),
+            *sems(2, 2, 2, 32, 16, 16, 16, 7, 7, 16, 16, 16, 16, 8, 8, 8, 8, 3),
             pltpu.VMEM((2, 640, 640), BF16),
             pltpu.VMEM((2, 640, 640), F32),
             pltpu.VMEM((2, 640, 640), F32),

time: 157 us -> 150 us (0.955)
  Pallas kernels: 152 us -> 144 us
    pallas_call x1, Pallas kernels: 148 us -> 141 us  [shampoo_step(): pl.pallas_call(step_kernel, out_shape=(jax.ShapeDtypeStruct((8, 8, 80, 64...]
where the time goes in v4:
time: 150 us; the launch traced here: 149 us
  Pallas kernels  144 us (96%)
  local copies, waits for them, and re-layouts  3.71 us (2%)
    pallas_call x1, Pallas kernels, shampoo_step(): pl.pallas_call(step_kernel, out_shape=(jax.ShapeDtypeStruct((8, 8, 80, 64...  141 us
    unnamed x8, local copies, waits for them, and re-layouts  3.71 us
    pallas_call x1, Pallas kernels, order_blocks(): pl.pallas_call(order_kernel, out_shape=(jax.ShapeDtypeStruct((8, 640, 640...  3.62 us

profile of v4, /device:TPU:4, one launch (start us, length us, event | category | flops | bytes accessed | tf_op | source)
XLA Modules:
  0.0 149.5 jit_solution(14744522141947463116)
XLA Ops:
  1.3 0.0 copy-start
  1.3 1.1 copy-done
  2.4 0.0 copy-start.1
  2.4 1.0 copy-done.1
  3.4 0.0 copy-start.2
  3.4 1.0 copy-done.2
  4.3 0.0 copy-start.3
  4.3 0.7 copy-done.3
  5.0 140.7 %shampoo_step.1 = (bf16[8,8,80,640]{3,2,1,0:T(8,128)(2,1)S(1)}, f32[160,640]{1,0:T(8,128)S(1)}, f32[160,640]{1,0:T(8,128)S(1)}) custom-call(bf16[256,640]{1,0:T(8,128)(2,1)S(1)} %copy-done.2, bf16[256,1280]{1,0:T(8,128)(2,1)S(1)} %copy-done, f32[160,640]{1,0:T(8,128)S(1)} %bitcast.6, s32[8]{0:T(128)S(1)} %copy-done.3, s32[1]{0:T(128)S(6)} %copy.8.rotation_ref), custom_call_target="tpu_custom_call" | custom-call | tf_op jit(solution)/shard_map/shampoo_step/pallas_call | solution.py:676
  145.7 3.6 %order_blocks.1 = (bf16[8,640,640]{2,1,0:T(8,128)(2,1)}, f32[160,640]{1,0:T(8,128)}, f32[160,640]{1,0:T(8,128)}) custom-call(s32[8]{0:T(128)S(1)} %copy-done.3, bf16[8,640,640]{2,1,0:T(8,128)(2,1)S(1)} %bitcast.5, f32[160,640]{1,0:T(8,128)S(1)} %get-tuple-element.10.stats_ref, f32[160,640]{1,0:T(8,128)S(1)} %get-tuple-element.11.roots_ref), custom_call_target="tpu_custom_call" | custom-call | tf_op jit(solution)/shard_map/order_blocks/pallas_call | solution.py:730
Async XLA Ops:
  1.3 1.1 copy-start
  2.4 1.0 copy-start.1
  3.4 1.0 copy-start.2
  4.3 0.7 copy-start.3

commit v5 on v4

--- a/solution.py
+++ b/solution.py
@@ -249,7 +249,6 @@
 
     x_copy(0).start()
     pl.when(root)(lambda: from_root(0))
-    y_send(0, OWN)
     stats.start(0)
     x_copy(1).start()
     keep = pltpu.make_async_copy(
@@ -261,6 +260,12 @@
     def _():
         actg[:, pl.ds(pl.multiple_of(group * 256, 256), 256)] = act_t[...]
 
+    @pl.when(stray)
+    def _():
+        a1_copy(0).wait_send()
+        a1_copy(1).wait_send()
+
+    y_send(0, OWN)
     pl.when(root)(lambda: from_root(1))
     x_landed(0)
     y_send(0, PAIR)
@@ -284,9 +289,7 @@
     pl.when(mid)(lambda: from_mid(2))
     stats.arrived(2)
     stats.start(3)
-    y_send(1, ON_OWN)
     pl.when(mid)(lambda: from_mid(3))
-    y_send(1, ON_PAIR)
 
     first = jnp.where(root, x_lo, other_x)
 
@@ -362,6 +365,8 @@
         return near
 
     sums0 = z_sum(0)
+    y_send(1, ON_OWN)
+    y_send(1, ON_PAIR)
     sums1 = z_sum(1)
     stats.arrived(3)
     spread0 = group_spread(0, sums0)
@@ -383,11 +388,6 @@
             for kind in range(4):
                 for way in range(2):
                     y_copy(chunk, kind, way).wait_send()
-
-        @pl.when(stray)
-        def _():
-            a1_copy(0).wait_send()
-            a1_copy(1).wait_send()
 
         @pl.when(same)
         def _():
@@ -570,28 +570,28 @@
     def across(g, index):
         send(update_ref.at[g, :, pl.ds(64, 16)], cs, index, partner)
 
-    near.start()
-    own_out(0)
     over = []
     for k in range(1, 8):
         own = update_ref.at[group, z, pl.ds(0, 32)]
         copy = remote(own, own, a_send.at[k], a_recv.at[k], g_peer[k - 1])
         copy.start()
         over.append(copy)
+    near.start()
+    own_out(0)
 
     own = dot(both[side, pl.ds(quarter, 160), :], both[1 - side])
     stats_out[...] = BETA * old_ref[...] + (1.0 - BETA) * own
     near.relay()
+    for copy in over:
+        copy.wait_recv()
+    ring_a.start(0)
+    ring_c.start(0)
     own_out(6)
     own_out(2)
     near.landed(2)
     own_out(7)
     near.landed(3)
     own_out(1)
-    for copy in over:
-        copy.wait_recv()
-    ring_a.start(0)
-    ring_c.start(0)
     pair_out(0)
     own_on(0)
     for r in (6, 2, 7, 1):
@@ -603,35 +603,35 @@
     near.landed(6)
     near.landed(7)
     own_out(4)
-    for r in (6, 2, 7, 1):
-        own_on(r)
     ring_a.arrived(0)
     ring_a.start(1)
     ring_c.arrived(0)
     ring_c.start(1)
+    for r in (6, 2, 7, 1):
+        own_on(r)
     for r in (5, 3, 4):
         pair_out(r)
     for r in (5, 3, 4):
         own_on(r)
+    ring_a.arrived(1)
+    ring_a.start(2)
+    ring_c.arrived(1)
+    ring_c.start(2)
     across(low, 0)
     across(high, 1)
     rot2[0] = rotated(1)
     rotate(2).start()
     for r in (0, 6, 2, 7, 1):
         pair_on(r)
-    ring_a.arrived(1)
-    ring_a.start(2)
-    ring_c.arrived(1)
-    ring_c.start(2)
+    ring_a.arrived(2)
+    ring_a.start(3)
+    ring_c.arrived(2)
+    ring_c.start(3)
     for r in (5, 3, 4):
         pair_on(r)
     for r in range(8):
         landed(rows(far, r, 32, 48), fs, r)
     across(far, 2)
-    ring_a.arrived(2)
-    ring_a.start(3)
-    ring_c.arrived(2)
-    ring_c.start(3)
     roots_out[...] = rotated(2).astype(F32)
     for r in range(8):
         landed(rows(p_far, r, 32, 32), qs, r)

time: 150 us -> 149 us (level)
  no operation moved by 1% of the time
where the time goes in v5:
time: 149 us; the launch traced here: 148 us
  Pallas kernels  143 us (96%)
  local copies, waits for them, and re-layouts  3.71 us (2%)
    pallas_call x1, Pallas kernels, shampoo_step(): pl.pallas_call(step_kernel, out_shape=(jax.ShapeDtypeStruct((8, 8, 80, 64...  139 us
    unnamed x8, local copies, waits for them, and re-layouts  3.71 us
    pallas_call x1, Pallas kernels, order_blocks(): pl.pallas_call(order_kernel, out_shape=(jax.ShapeDtypeStruct((8, 640, 640...  3.62 us

profile of v5, /device:TPU:4, one launch (start us, length us, event | category | flops | bytes accessed | tf_op | source)
XLA Modules:
  0.0 148.1 jit_solution(6212765215863561362)
XLA Ops:
  1.3 0.0 copy-start
  1.3 1.1 copy-done
  2.4 0.0 copy-start.1
  2.4 1.0 copy-done.1
  3.4 0.0 copy-start.2
  3.4 1.0 copy-done.2
  4.3 0.0 copy-start.3
  4.3 0.7 copy-done.3
  5.0 139.3 %shampoo_step.1 = (bf16[8,8,80,640]{3,2,1,0:T(8,128)(2,1)S(1)}, f32[160,640]{1,0:T(8,128)S(1)}, f32[160,640]{1,0:T(8,128)S(1)}) custom-call(bf16[256,640]{1,0:T(8,128)(2,1)S(1)} %copy-done.2, bf16[256,1280]{1,0:T(8,128)(2,1)S(1)} %copy-done, f32[160,640]{1,0:T(8,128)S(1)} %bitcast.6, s32[8]{0:T(128)S(1)} %copy-done.3, s32[1]{0:T(128)S(6)} %copy.8.rotation_ref), custom_call_target="tpu_custom_call" | custom-call | tf_op jit(solution)/shard_map/shampoo_step/pallas_call | solution.py:676
  144.3 3.6 %order_blocks.1 = (bf16[8,640,640]{2,1,0:T(8,128)(2,1)}, f32[160,640]{1,0:T(8,128)}, f32[160,640]{1,0:T(8,128)}) custom-call(s32[8]{0:T(128)S(1)} %copy-done.3, bf16[8,640,640]{2,1,0:T(8,128)(2,1)S(1)} %bitcast.5, f32[160,640]{1,0:T(8,128)S(1)} %get-tuple-element.10.stats_ref, f32[160,640]{1,0:T(8,128)S(1)} %get-tuple-element.11.roots_ref), custom_call_target="tpu_custom_call" | custom-call | tf_op jit(solution)/shard_map/order_blocks/pallas_call | solution.py:730
Async XLA Ops:
  1.3 1.1 copy-start
  2.4 1.0 copy-start.1
  3.4 1.0 copy-start.2
  4.3 0.7 copy-start.3

commit v6 on v5

--- a/solution.py
+++ b/solution.py
@@ -744,6 +744,10 @@
 
 def local(activations, grad_out, stats_old, owner_map, rotation):
     old_rows = stats_old.reshape(160, 640)
+    activations, grad_out, old_rows = (
+        pltpu.with_memory_space_constraint(x, pltpu.HBM)
+        for x in (activations, grad_out, old_rows)
+    )
     by_place, stats_new, roots_new = shampoo_step(
         activations, grad_out, old_rows, owner_map, rotation
     )

time: 149 us -> 145 us (0.973)
  local copies, waits for them, and re-layouts: 3.71 us -> 0.65 us
    unnamed x8 -> x2, local copies, waits for them, and re-layouts: 3.71 us -> 0.65 us
where the time goes in v6:
time: 145 us
  Pallas kernels  143 us (99%)
  between operations  1.45 us (1%)
    pallas_call x1, Pallas kernels, shampoo_step(): pl.pallas_call(step_kernel, out_shape=(jax.ShapeDtypeStruct((8, 8, 80, 64...  139 us
    pallas_call x1, Pallas kernels, order_blocks(): pl.pallas_call(order_kernel, out_shape=(jax.ShapeDtypeStruct((8, 640, 640...  3.62 us

profile of v6, /device:TPU:4, one launch (start us, length us, event | category | flops | bytes accessed | tf_op | source)
XLA Modules:
  0.0 144.6 jit_solution(2202981069380900450)
XLA Ops:
  1.3 0.0 copy-start
  1.3 0.6 copy-done
  1.9 138.9 %shampoo_step.1 = (bf16[8,8,80,640]{3,2,1,0:T(8,128)(2,1)S(1)}, f32[160,640]{1,0:T(8,128)S(1)}, f32[160,640]{1,0:T(8,128)S(1)}) custom-call(bf16[256,640]{1,0:T(8,128)(2,1)} %act_ref.1, bf16[256,1280]{1,0:T(8,128)(2,1)} %gout_ref.1, f32[160,640]{1,0:T(8,128)} %bitcast.6, s32[8]{0:T(128)S(1)} %copy-done, s32[1]{0:T(128)S(6)} %copy.8.rotation_ref), custom_call_target="tpu_custom_call" | custom-call | tf_op jit(solution)/shard_map/shampoo_step/pallas_call | solution.py:676
  140.9 3.6 %order_blocks.1 = (bf16[8,640,640]{2,1,0:T(8,128)(2,1)}, f32[160,640]{1,0:T(8,128)}, f32[160,640]{1,0:T(8,128)}) custom-call(s32[8]{0:T(128)S(1)} %copy-done, bf16[8,640,640]{2,1,0:T(8,128)(2,1)S(1)} %bitcast.5, f32[160,640]{1,0:T(8,128)S(1)} %get-tuple-element.10.stats_ref, f32[160,640]{1,0:T(8,128)S(1)} %get-tuple-element.11.roots_ref), custom_call_target="tpu_custom_call" | custom-call | tf_op jit(solution)/shard_map/order_blocks/pallas_call | solution.py:730
Async XLA Ops:
  1.3 0.7 copy-start

commit v7 on v6

--- a/solution.py
+++ b/solution.py
@@ -715,10 +715,16 @@
 
 def order_kernel(owner_ref, in_ref, stats_ref, roots_ref, out_ref, stats_out, roots_out, sems):
     copies = [
-        pltpu.make_async_copy(in_ref.at[owner_ref[b]], out_ref.at[b], sems.at[b]) for b in range(8)
+        pltpu.make_async_copy(
+            in_ref.at[owner_ref[b], pl.ds(half * 320, 320)],
+            out_ref.at[b, pl.ds(half * 320, 320)],
+            sems.at[b * 2 + half],
+        )
+        for b in range(8)
+        for half in range(2)
     ]
-    copies.append(pltpu.make_async_copy(stats_ref, stats_out, sems.at[8]))
-    copies.append(pltpu.make_async_copy(roots_ref, roots_out, sems.at[9]))
+    copies.append(pltpu.make_async_copy(stats_ref, stats_out, sems.at[16]))
+    copies.append(pltpu.make_async_copy(roots_ref, roots_out, sems.at[17]))
     for copy in copies:
         copy.start()
     for copy in copies:
@@ -736,7 +742,7 @@
         ),
         in_specs=[SMEM, VMEM, VMEM, VMEM],
         out_specs=(hbm, hbm, hbm),
-        scratch_shapes=[pltpu.SemaphoreType.DMA((10,))],
+        scratch_shapes=[pltpu.SemaphoreType.DMA((18,))],
         compiler_params=pltpu.CompilerParams(vmem_limit_bytes=16 * 2**20),
         name="order_blocks",
     )(owner_map, by_place, stats_new, roots_new)

time: 145 us -> 145 us (level)
  no operation moved by 1% of the time
where the time goes in v7:
time: 145 us
  Pallas kernels  143 us (99%)
  between operations  1.45 us (1%)
    pallas_call x1, Pallas kernels, shampoo_step(): pl.pallas_call(step_kernel, out_shape=(jax.ShapeDtypeStruct((8, 8, 80, 64...  139 us
    pallas_call x1, Pallas kernels, order_blocks(): pl.pallas_call(order_kernel, out_shape=(jax.ShapeDtypeStruct((8, 640, 640...  3.68 us

profile of v7, /device:TPU:4, one launch (start us, length us, event | category | flops | bytes accessed | tf_op | source)
XLA Modules:
  0.0 144.7 jit_solution(5323937085898745801)
XLA Ops:
  1.3 0.0 copy-start
  1.3 0.6 copy-done
  1.9 138.9 %shampoo_step.1 = (bf16[8,8,80,640]{3,2,1,0:T(8,128)(2,1)S(1)}, f32[160,640]{1,0:T(8,128)S(1)}, f32[160,640]{1,0:T(8,128)S(1)}) custom-call(bf16[256,640]{1,0:T(8,128)(2,1)} %act_ref.1, bf16[256,1280]{1,0:T(8,128)(2,1)} %gout_ref.1, f32[160,640]{1,0:T(8,128)} %bitcast.6, s32[8]{0:T(128)S(1)} %copy-done, s32[1]{0:T(128)S(6)} %copy.8.rotation_ref), custom_call_target="tpu_custom_call" | custom-call | tf_op jit(solution)/shard_map/shampoo_step/pallas_call | solution.py:676
  140.9 3.7 %order_blocks.1 = (bf16[8,640,640]{2,1,0:T(8,128)(2,1)}, f32[160,640]{1,0:T(8,128)}, f32[160,640]{1,0:T(8,128)}) custom-call(s32[8]{0:T(128)S(1)} %copy-done, bf16[8,640,640]{2,1,0:T(8,128)(2,1)S(1)} %bitcast.5, f32[160,640]{1,0:T(8,128)S(1)} %get-tuple-element.10.stats_ref, f32[160,640]{1,0:T(8,128)S(1)} %get-tuple-element.11.roots_ref), custom_call_target="tpu_custom_call" | custom-call | tf_op jit(solution)/shard_map/order_blocks/pallas_call | solution.py:736
Async XLA Ops:
  1.3 0.7 copy-start
